TPU v7x, 32 devices: a whole 2x2x4 slice. The times are simulated.
32 devices in a mesh: group: 4 (over x, core), tp: 8 (over z, y).
Axes of the slice: x: 2, y: 2, z: 4, core: 2. Of those that a mesh axis runs over, the one named last changes fastest.
Arguments:
- prefill_x: bfloat16 [512, 16384], P('group', 'tp'), may hold values from -6 to 6
- prefill_gate: bfloat16 [512, 16384], P('group', 'tp'), may hold values from -6 to 6
- lengths: int32 [4, 8], P('group'), may hold values from 1 to 64, 128 in all within a row
- routes: int32 [32, 1], replicated, may hold values from 0 to 3; in each aligned block of 8 rows (0 to 7, 8 to 15, ...) at most 4 rows name the same one
- decode_x: bfloat16 [4, 128, 16384], P(None, 'group', 'tp'), may hold values from -6 to 6
- decode_gate: bfloat16 [4, 128, 16384], P(None, 'group', 'tp'), may hold values from -6 to 6
- cached_state: float32 [128, 16, 16384], P('group', None, 'tp'), may hold values from -4 to 4
- xproj_weight: bfloat16 [16384, 544], P('tp'), may hold values from -0.046875 to 0.046875
- dt_weight: bfloat16 [512, 16384], P(None, 'tp'), may hold values from -0.25 to 0.25
- dt_bias: float32 [16384], P('tp'), may hold values from -3 to -1
- a_log: float32 [16, 16384], P(None, 'tp'), may hold values from 0 to 2.77
- skip_gain: float32 [16384], P('tp'), may hold values from 0.5 to 1.5
Outputs:
- prefill_out: bfloat16 [512, 16384], P('group', 'tp')
- decode_out: bfloat16 [4, 128, 16384], P(None, 'group', 'tp')
Inputs may be any that keep to these rules, and one draw needn't show every extreme that they name: `routes`: in each aligned block of 8 rows (the requests of one group) no decode group is named more than 4 times. `lengths`: each group's row sums to 128; its largest entry is 64.
All inputs are finite; a program needn't handle non-finite values.
Results may differ from a plain program's by a relative error of at most 0.0051.
Values sent between devices are 32-bit elements; how exact they have to be, the bound alone decides.
A program may use at most 128 MiB of HBM per device.

v0:
```python
import jax
import jax.numpy as jnp
from jax import lax
from jax.sharding import PartitionSpec as P


def project_columns(inputs, xproj_weight):
    return lax.dot_general(
        xproj_weight, inputs, (((0,), (1,)), ((), ())), preferred_element_type=jnp.float32
    )


def mixer_terms(projected, dt_weight, dt_bias, state_width):
    low_rank = dt_weight.shape[0]
    low_part = projected[:low_rank].astype(jnp.bfloat16)
    step_size = jax.nn.softplus(
        lax.dot_general(
            low_part, dt_weight, (((0,), (0,)), ((), ())), preferred_element_type=jnp.float32
        )
        + dt_bias
    )
    vectors = jnp.transpose(projected[low_rank:])
    return (step_size, vectors[:, :state_width], vectors[:, state_width:])


def combine(earlier, latter):
    return (earlier[0] * latter[0], latter[0] * earlier[1] + latter[1])


def gated_output(hidden, readout, values, skip_gain, gate_rows):
    mixed = jnp.sum(readout[:, :, None] * hidden, axis=1)
    return ((mixed + skip_gain * values) * jax.nn.silu(gate_rows.astype(jnp.float32))).astype(
        jnp.bfloat16
    )


def local(
    prefill_x,
    prefill_gate,
    lengths,
    routes,
    decode_x,
    decode_gate,
    cached_state,
    xproj_weight,
    dt_weight,
    dt_bias,
    a_log,
    skip_gain,
):
    state_width = a_log.shape[0]
    channels = prefill_x.shape[1]
    tokens = prefill_x.shape[0]
    row_count = cached_state.shape[0]
    step_count = decode_x.shape[0]
    group_index = lax.axis_index("group")
    rates = -jnp.exp(a_log)
    prefill_part = project_columns(prefill_x, xproj_weight)
    decode_part = project_columns(decode_x.reshape(step_count * row_count, channels), xproj_weight)
    prefill_proj = lax.psum(prefill_part, "tp")
    decode_proj = lax.psum(decode_part, "tp")
    step_size, inject, readout = mixer_terms(prefill_proj, dt_weight, dt_bias, state_width)
    lengths_here = lengths[0]
    request_end = jnp.cumsum(lengths_here) - 1
    request_start = request_end - lengths_here + 1
    block_size = min(256, tokens)
    carried = jnp.zeros((state_width, channels), jnp.float32)
    position = 0 + jnp.arange(block_size, dtype=jnp.int32)
    first_token = jnp.any(position[:, None] == request_start[None, :], axis=1)
    survive = jnp.where(first_token, jnp.float32(0.0), jnp.float32(1.0))
    values = prefill_x.astype(jnp.float32)
    damping = survive[:, None, None] * jnp.exp(step_size[:, None, :] * rates[None])
    forcing = step_size[:, None, :] * inject[0:block_size, :, None] * values[:, None, :]
    prefix_damping, prefix_forcing = lax.associative_scan(combine, (damping, forcing), axis=0)
    hidden = prefix_damping * carried[None] + prefix_forcing
    pieces = gated_output(hidden, readout, values, skip_gain, prefill_gate)
    selector = (request_end[:, None] == position[None, :]).astype(jnp.float32)
    final_states = jnp.einsum("kt,tse->kse", selector, hidden, precision=lax.Precision.HIGHEST)
    flat_routes = routes[:, 0]
    total_requests = flat_routes.shape[0]
    ordering = jnp.arange(total_requests, dtype=jnp.int32)
    same_dest = flat_routes[:, None] == flat_routes[None, :]
    slot_index = jnp.sum(
        ((ordering[:, None] > ordering[None, :]) & same_dest).astype(jnp.int32), axis=1
    )
    destinations = flat_routes * row_count + slot_index
    row_ids = group_index * row_count + jnp.arange(row_count, dtype=jnp.int32)
    state_pool = lax.all_gather(final_states, "group", axis=0, tiled=True)
    matches = row_ids[:, None] == destinations[None, :]
    arrived = jnp.any(matches, axis=1)
    source = jnp.argmax(matches.astype(jnp.int32), axis=1)
    hidden = jnp.where(arrived[:, None, None], state_pool[source], cached_state)
    step_all, inject_all, readout_all = mixer_terms(decode_proj, dt_weight, dt_bias, state_width)
    step_all = step_all.reshape(step_count, row_count, channels)
    inject_all = inject_all.reshape(step_count, row_count, state_width)
    readout_all = readout_all.reshape(step_count, row_count, state_width)
    results = []
    for step_index in range(step_count):
        step_now = step_all[step_index]
        values = decode_x[step_index].astype(jnp.float32)
        hidden = (
            jnp.exp(step_now[:, None, :] * rates[None]) * hidden
            + step_now[:, None, :] * inject_all[step_index][:, :, None] * values[:, None, :]
        )
        results.append(
            gated_output(
                hidden, readout_all[step_index], values, skip_gain, decode_gate[step_index]
            )
        )
    decode_out = jnp.stack(results)
    return (pieces, decode_out)


def solution(mesh):
    placed = (
        P("group", "tp"),
        P("group", "tp"),
        P("group", None),
        P(),
        P(None, "group", "tp"),
        P(None, "group", "tp"),
        P("group", None, "tp"),
        P("tp", None),
        P(None, "tp"),
        P("tp"),
        P(None, "tp"),
        P("tp"),
    )
    return jax.shard_map(
        local,
        mesh=mesh,
        in_specs=placed,
        out_specs=(P("group", "tp"), P(None, "group", "tp")),
        check_vma=False,
    )
```

profile of v0, /device:TPU:13, one launch (start us, length us, event | category | flops | bytes accessed | tf_op | source)
XLA Modules:
  0.0 1047.6 jit_solution(10468985940160974863)
XLA Ops:
  13.9 71.4 %all-reduce.31.cloned.1.call-done = (f32[544,128]{1,0:T(8,128)}, f32[544,128]{1,0:T(8,128)}) async-done(((f32[544,128]{1,0:T(8,128)}, f32[544,128]{1,0:T(8,128)}), (f32[544,128]{1,0:T(8,128)}, f32[544,128]{1,0:T(8,128)})) %all-reduce.31.cloned.1.call-update) | async-done | bytes 557072 | tf_op jit(solution)/shard_map/psum | solution.py:60
  89.8 7.2 exponential_multiply_fusion
  103.5 36.8 %slice.336 = f32[63,16,2048]{2,0,1:T(8,128)} slice(f32[128,16,2048]{2,0,1:T(8,128)} %copy-done.2), slice={[2:128:2], [0:16:1], [0:2048:1]} | slice | bytes 16515072 | tf_op jit(solution)/shard_map/slice | solution.py:74
  140.3 36.0 %slice.307 = f32[64,16,2048]{2,0,1:T(8,128)} slice(f32[128,16,2048]{2,0,1:T(8,128)} %copy-done.2), slice={[1:128:2], [0:16:1], [0:2048:1]} | slice | bytes 16777216 | tf_op jit(solution)/shard_map/slice | solution.py:74
  176.3 36.0 %slice.306 = f32[64,16,2048]{2,0,1:T(8,128)} slice(f32[128,16,2048]{2,0,1:T(8,128)} %copy-done.2), slice={[0:127:2], [0:16:1], [0:2048:1]} | slice | bytes 16777216 | tf_op jit(solution)/shard_map/slice | solution.py:74
  214.3 36.8 %slice.369 = f32[63,16,2048]{2,0,1:T(8,128)} slice(f32[128,16,2048]{2,0,1:T(8,128)} %get-tuple-element.37), slice={[2:128:2], [0:16:1], [0:2048:1]} | slice | bytes 16515072 | tf_op jit(solution)/shard_map/slice | solution.py:74
  251.0 36.0 %slice.340 = f32[64,16,2048]{2,0,1:T(8,128)} slice(f32[128,16,2048]{2,0,1:T(8,128)} %get-tuple-element.37), slice={[1:128:2], [0:16:1], [0:2048:1]} | slice | bytes 16777216 | tf_op jit(solution)/shard_map/slice | solution.py:74
  287.0 36.0 %slice.339 = f32[64,16,2048]{2,0,1:T(8,128)} slice(f32[128,16,2048]{2,0,1:T(8,128)} %get-tuple-element.37), slice={[0:127:2], [0:16:1], [0:2048:1]} | slice | bytes 16777216 | tf_op jit(solution)/shard_map/slice | solution.py:74
  323.0 19.0 %fusion.47 = (f32[64,16,2048]{2,0,1:T(8,128)}, f32[64,16,2048]{2,0,1:T(8,128)}) fusion(f32[64,16,2048]{2,0,1:T(8,128)} %slice.306, f32[64,16,2048]{2,0,1:T(8,128)} %slice.307, f32[64,16,2048]{2,0,1:T(8,128)} %slice.340, f32[64,16,2048]{2,0,1:T(8,128)} %slice.339), kind=kLoop, calls=%fused_computation.136 | loop fusion | flops 6291456 | bytes 50331648 | tf_op jit(solution)/shard_map/mul | solution.py:27
  343.3 18.9 %slice.334 = f32[31,16,2048]{2,0,1:T(8,128)} slice(f32[64,16,2048]{2,0,1:T(8,128)} %get-tuple-element.14), slice={[2:64:2], [0:16:1], [0:2048:1]} | slice | bytes 8126464 | tf_op jit(solution)/shard_map/slice | solution.py:74
  362.2 18.5 %slice.310 = f32[32,16,2048]{2,0,1:T(8,128)} slice(f32[64,16,2048]{2,0,1:T(8,128)} %get-tuple-element.14), slice={[1:64:2], [0:16:1], [0:2048:1]} | slice | bytes 8388608 | tf_op jit(solution)/shard_map/slice | solution.py:74
  380.6 18.5 %slice.309 = f32[32,16,2048]{2,0,1:T(8,128)} slice(f32[64,16,2048]{2,0,1:T(8,128)} %get-tuple-element.14), slice={[0:63:2], [0:16:1], [0:2048:1]} | slice | bytes 8388608 | tf_op jit(solution)/shard_map/slice | solution.py:74
  401.1 18.8 %slice.367 = f32[31,16,2048]{2,0,1:T(8,128)} slice(f32[64,16,2048]{2,0,1:T(8,128)} %get-tuple-element.15), slice={[2:64:2], [0:16:1], [0:2048:1]} | slice | bytes 8126464 | tf_op jit(solution)/shard_map/slice | solution.py:74
  420.0 18.5 %slice.343 = f32[32,16,2048]{2,0,1:T(8,128)} slice(f32[64,16,2048]{2,0,1:T(8,128)} %get-tuple-element.15), slice={[1:64:2], [0:16:1], [0:2048:1]} | slice | bytes 8388608 | tf_op jit(solution)/shard_map/slice | solution.py:74
  438.5 18.5 %slice.342 = f32[32,16,2048]{2,0,1:T(8,128)} slice(f32[64,16,2048]{2,0,1:T(8,128)} %get-tuple-element.15), slice={[0:63:2], [0:16:1], [0:2048:1]} | slice | bytes 8388608 | tf_op jit(solution)/shard_map/slice | solution.py:74
  456.9 10.2 fusion.48
  469.8 9.9 slice.332
  479.7 9.8 slice.313
  489.5 9.8 slice.312
  501.2 9.9 slice.365
  511.1 9.8 slice.346
  520.9 9.8 slice.345
  591.8 9.5 pad.105
  610.0 10.4 pad.92
  620.3 10.5 %pad.93 = f32[16,16,2048]{2,0,1:T(8,128)} pad(f32[8,16,2048]{2,0,1:T(8,128)} %add.261, f32[]{:T(128)} %constant.35.clone.1), padding=1_0_1x0_0_0x0_0_0 | pad | bytes 3145732 | tf_op jit(solution)/shard_map/pad | solution.py:74
  630.8 6.9 pad.107
  647.8 8.0 pad.108
  657.8 8.1 pad.94
  665.9 12.1 %pad.95 = f32[32,16,2048]{2,0,1:T(8,128)} pad(f32[16,16,2048]{2,0,1:T(8,128)} %add.262, f32[]{:T(128)} %constant.35.clone.1), padding=1_0_1x0_0_0x0_0_0 | pad | bytes 6291460 | tf_op jit(solution)/shard_map/pad | solution.py:74
  677.9 8.0 pad.109
  685.9 6.7 add.281
  697.6 7.0 add_multiply_fusion.3
  709.6 14.3 %pad.110 = f32[64,16,2048]{2,0,1:T(8,128)} pad(f32[32,16,2048]{2,0,1:T(8,128)} %pad_maximum_fusion.3, f32[]{:T(128)} %constant.35.clone.1), padding=0_1_1x0_0_0x0_0_0 | pad | bytes 12582916 | tf_op jit(solution)/shard_map/pad | solution.py:74
  729.0 14.3 %pad.96 = f32[64,16,2048]{2,0,1:T(8,128)} pad(f32[32,16,2048]{2,0,1:T(8,128)} %pad_maximum_fusion.2, f32[]{:T(128)} %constant.35.clone.1), padding=0_1_1x0_0_0x0_0_0 | pad | bytes 12582916 | tf_op jit(solution)/shard_map/pad | solution.py:74
  743.4 14.3 %pad.97 = f32[64,16,2048]{2,0,1:T(8,128)} pad(f32[32,16,2048]{2,0,1:T(8,128)} %add.263, f32[]{:T(128)} %constant.35.clone.1), padding=1_0_1x0_0_0x0_0_0 | pad | bytes 12582916 | tf_op jit(solution)/shard_map/pad | solution.py:74
  757.7 14.8 %pad.111 = f32[64,16,2048]{2,0,1:T(8,128)} pad(f32[32,16,2048]{2,0,1:T(8,128)} %add.281, f32[]{:T(128)} %constant.35.clone.1), padding=1_0_1x0_0_0x0_0_0 | pad | bytes 12582916 | tf_op jit(solution)/shard_map/pad | solution.py:74
  772.4 11.7 %add.283 = f32[64,16,2048]{2,0,1:T(8,128)} add(f32[64,16,2048]{2,0,1:T(8,128)} %pad.110, f32[64,16,2048]{2,0,1:T(8,128)} %pad.111) | non-fusion elementwise | flops 2097152 | bytes 25165824 | tf_op jit(solution)/shard_map/add | solution.py:74
  784.2 11.7 %add.264 = f32[64,16,2048]{2,0,1:T(8,128)} add(f32[64,16,2048]{2,0,1:T(8,128)} %pad.96, f32[64,16,2048]{2,0,1:T(8,128)} %pad.97) | non-fusion elementwise | flops 2097152 | bytes 25165824 | tf_op jit(solution)/shard_map/add | solution.py:74
  795.9 20.8 %add_multiply_fusion.1 = (f32[63,16,2048]{2,0,1:T(8,128)}, f32[63,16,2048]{2,0,1:T(8,128)S(1)}) fusion(f32[63,16,2048]{2,0,1:T(8,128)} %slice.336, f32[64,16,2048]{2,0,1:T(8,128)} %pad.97, f32[64,16,2048]{2,0,1:T(8,128)} %pad.96, f32[63,16,2048]{2,0,1:T(8,128)} %slice.369, f32[64,16,2048]{2,0,1:T(8,128)} %pad.111, f32[64,16,2048]{2,0,1:T(8,128)} %pad.110), kind=kLoop, calls=%fused_computation.7 | loop fusion | flops 10321920 | bytes 66060288 | tf_op jit(solution)/shard_map/mul | solution.py:27
  821.1 27.9 %pad.112 = f32[128,16,2048]{2,0,1:T(8,128)} pad(f32[64,16,2048]{2,0,1:T(8,128)} %pad_maximum_fusion.1, f32[]{:T(128)} %constant.35.clone.1), padding=0_1_1x0_0_0x0_0_0 | pad | bytes 25165828 | tf_op jit(solution)/shard_map/pad | solution.py:74
  849.0 8.6 pad_maximum_fusion
  857.6 27.9 %pad.98 = f32[128,16,2048]{2,0,1:T(8,128)} pad(f32[64,16,2048]{2,0,1:T(8,128)} %pad_maximum_fusion, f32[]{:T(128)} %constant.35.clone.1), padding=0_1_1x0_0_0x0_0_0 | pad | bytes 25165828 | tf_op jit(solution)/shard_map/pad | solution.py:74
  885.5 27.9 %pad.99 = f32[128,16,2048]{2,0,1:T(8,128)} pad(f32[64,16,2048]{2,0,1:T(8,128)} %add.264, f32[]{:T(128)} %constant.35.clone.1), padding=1_0_1x0_0_0x0_0_0 | pad | bytes 25165828 | tf_op jit(solution)/shard_map/pad | solution.py:74
  913.4 27.9 %pad.113 = f32[128,16,2048]{2,0,1:T(8,128)} pad(f32[64,16,2048]{2,0,1:T(8,128)} %add.283, f32[]{:T(128)} %constant.35.clone.1), padding=1_0_1x0_0_0x0_0_0 | pad | bytes 25165828 | tf_op jit(solution)/shard_map/pad | solution.py:74
  941.3 29.6 %multiply_reduce_fusion = (f32[128,2048]{1,0:T(8,128)S(1)}, f32[128,16,2048]{2,0,1:T(8,128)}) fusion(f32[128,16]{0,1:T(8,128)S(1)} %copy-done.40, f32[128,16,2048]{2,0,1:T(8,128)} %pad.112, f32[128,16,2048]{2,0,1:T(8,128)} %pad.113, f32[128,16,2048]{2,0,1:T(8,128)} %pad.98, f32[128,16,2048]{2,0,1:T(8,128)} %pad.99), kind=kLoop, calls=%fused_computation.1 | loop fusion | flops 24903680 | bytes 84942848 | tf_op jit(solution)/shard_map/reduce_sum | solution.py:31
  970.9 10.0 fusion.42
  988.5 28.3 %all-gather.2.cloned.1.call-done = f32[32,16,2048]{2,0,1:T(8,128)} async-done(((f32[8,16,2048]{2,0,1:T(8,128)}), f32[32,16,2048]{2,0,1:T(8,128)}) %all-gather.2.cloned.1.call-update) | async-done | bytes 4194320 | tf_op jit(solution)/shard_map/all_gather | solution.py:88
  1028.4 10.9 %multiply_reduce_fusion.2 = (f32[32,2048]{1,0:T(8,128)S(1)}, f32[32,2048]{1,0:T(8,128)S(1)}, f32[32,2048]{1,0:T(8,128)S(1)}, f32[32,2048]{1,0:T(8,128)S(1)}) fusion(f32[32,16]{1,0:T(8,128)S(1)} %copy.29, f32[32,2048]{1,0:T(8,128)} %get-tuple-element.41, f32[32,16]{1,0:T(8,128)S(1)} %copy.30, f32[32,2048]{1,0:T(8,128)S(1)} %get-tuple-element.39, ...), kind=kLoop, calls=%fused_computation.17 | loop fusion | flops 30146560 | bytes 11681824 | tf_op jit(solution)/shard_map/reduce_sum | solution.py:31
  (194 shorter events, 149.0 us)
Async XLA Ops:
  7.2 1.6 copy-start
  7.2 4.1 copy-start.16
  7.2 78.1 %all-reduce.31.cloned.1.call-start = ((), (), s32[]{:S(2)}) async-start(), calls=%async_computation.1 | async-start | bytes 1114112 | tf_op jit(solution)/shard_map/psum | solution.py:60
  11.3 1.5 copy-start.45
  11.3 2.5 copy-start.38
  11.3 75.9 %copy-start.43 = (f32[2048]{0:T(1024)S(1)}, f32[2048]{0:T(1024)}, u32[]{:S(2)}) copy-start(f32[2048]{0:T(1024)} %param.21) | copy-start | bytes 24580
  12.8 1004.0 %all-gather.2.cloned.1.call-start = ((), (), s32[]{:S(2)}) async-start(), calls=%async_computation | async-start | bytes 5242880 | tf_op jit(solution)/shard_map/all_gather | solution.py:88
  13.9 83.2 %copy-start.24 = (f32[16,2048]{1,0:T(8,128)}, f32[16,2048]{1,0:T(8,128)S(1)}, u32[]{:S(2)}) copy-start(f32[16,2048]{1,0:T(8,128)S(1)} %exponential_negate_fusion) | copy-start | bytes 393220
  97.1 5.7 copy-start.2
  467.1 2.0 copy-start.7
  535.1 1.3 copy-start.11
  576.3 5.6 copy-start.22
  576.3 5.6 copy-start.23
  579.9 3.3 copy-start.36
  580.9 2.9 copy-start.35
  601.3 3.7 copy-start.12
  601.3 3.7 copy-start.20
  601.3 3.7 copy-start.21
  604.9 1.6 copy-start.34
  606.5 0.9 copy-start.33
  607.4 23.4 %copy-start.19 = (f32[8,16,2048]{2,0,1:T(8,128)S(1)}, f32[8,16,2048]{2,0,1:T(8,128)}, u32[]{:S(2)}) copy-start(f32[8,16,2048]{2,0,1:T(8,128)} %add.277) | copy-start | bytes 3145732
  637.7 3.4 copy-start.8
  637.7 3.4 copy-start.9
  641.1 2.3 copy-start.10
  641.1 3.0 copy-start.14
  641.2 3.6 copy-start.15
  644.8 2.7 copy-start.32
  647.8 8.0 copy-start.31
  665.9 12.1 %copy-start.13 = (f32[16,16,2048]{2,0,1:T(8,128)S(1)}, f32[16,16,2048]{2,0,1:T(8,128)}, u32[]{:S(2)}) copy-start(f32[16,16,2048]{2,0,1:T(8,128)} %add.279) | copy-start | bytes 6291460
  685.9 6.7 copy-start.4
  685.9 6.7 copy-start.5
  692.6 3.3 copy-start.3
  692.6 5.0 copy-start.6
  697.6 7.0 copy-start.28
  795.9 20.8 %copy-start.27 = (f32[1,16,2048]{2,0,1:T(1,128)S(1)}, f32[1,16,2048]{2,0,1:T(1,128)}, u32[]{:S(2)}) copy-start(f32[1,16,2048]{2,0,1:T(1,128)} %slice.419) | copy-start | bytes 393220
  821.1 27.9 %copy-start.26 = (f32[1,16,2048]{2,0,1:T(1,128)S(1)}, f32[1,16,2048]{2,0,1:T(1,128)}, u32[]{:S(2)}) copy-start(f32[1,16,2048]{2,0,1:T(1,128)} %slice.397) | copy-start | bytes 393220
  913.4 27.9 %copy-start.40 = (f32[128,16]{0,1:T(8,128)S(1)}, f32[128,16]{0,1:T(8,128)}, u32[]{:S(2)}) copy-start(f32[128,16]{0,1:T(8,128)} %get-tuple-element.65) | copy-start | bytes 24580
  941.3 29.6 %copy-start.41 = (s32[8]{0:T(128)S(1)}, s32[8]{0:T(128)}, u32[]{:S(2)}) copy-start(s32[8]{0:T(128)} %add_bitcast_fusion) | copy-start | bytes 100
  970.9 10.1 copy-start.42
  970.9 11.2 %copy-start.18 = (bf16[4,32,2048]{2,1,0:T(8,128)(2,1)S(1)}, bf16[4,32,2048]{2,1,0:T(8,128)(2,1)}, u32[]{:S(2)}) copy-start(bf16[4,32,2048]{2,1,0:T(8,128)(2,1)} %param.16) | copy-start | bytes 1572868
  970.9 12.1 %copy-start.37 = (f32[128,32]{0,1:T(8,128)S(1)}, f32[128,32]{0,1:T(8,128)}, u32[]{:S(2)}) copy-start(f32[128,32]{0,1:T(8,128)} %get-tuple-element.66) | copy-start | bytes 49156
  970.9 12.8 %copy-start.44 = (f32[2048]{0:T(1024)S(1)}, f32[2048]{0:T(1024)}, u32[]{:S(2)}) copy-start(f32[2048]{0:T(1024)} %param.21) | copy-start | bytes 24580
  980.9 6.4 copy-start.17
  980.9 6.4 copy-start.29
  980.9 6.3 copy-start.39
  1023.4 5.0 copy-start.25
  1028.4 10.9 %copy-start.30 = (bf16[4,32,2048]{2,1,0:T(8,128)(2,1)S(1)}, bf16[4,32,2048]{2,1,0:T(8,128)(2,1)}, u32[]{:S(2)}) copy-start(bf16[4,32,2048]{2,1,0:T(8,128)(2,1)} %param.17) | copy-start | bytes 1572868
  1028.4 12.2 %copy-start.1 = (bf16[2048,544]{0,1:T(8,128)(2,1)S(1)}, bf16[2048,544]{0,1:T(8,128)(2,1)}, u32[]{:S(2)}) copy-start(bf16[2048,544]{0,1:T(8,128)(2,1)} %param.19) | copy-start | bytes 6684676
Sparse Core Ops, SparseCore 0:
  12.9 72.2 all-reduce.30
  981.0 35.6 all-gather.1
where the time goes:
time: 1070 us; the launch traced here: 1050 us
  local copies, waits for them, and re-layouts  714 us (67%)
  other arithmetic  200 us (19%)
  waiting for transfers between devices  99.7 us (9%)
  matrix products  19.2 us (2%)
  between operations  14.8 us (1%)
    slice x44, local copies, waits for them, and re-layouts, local(): lax.associative_scan(combine, (damping, forcing), axis=0)  432 us
    pad x24, local copies, waits for them, and re-layouts, local(): lax.associative_scan(combine, (damping, forcing), axis=0)  252 us
    psum x1, waiting for transfers between devices, local(): prefill_proj = lax.psum(prefill_part, 'tp')  71.4 us
    mul x12, other arithmetic, combine(): return (earlier[0] * latter[0], latter[0] * earlier[1] + latter[1])  69.8 us
    add x12, other arithmetic, local(): lax.associative_scan(combine, (damping, forcing), axis=0)  44.1 us
    reduce_sum x2, other arithmetic, gated_output(): mixed = jnp.sum(readout[:, :, None] * hidden, axis=1)  40.5 us
    concatenate x12, other arithmetic, local(): lax.associative_scan(combine, (damping, forcing), axis=0)  31.1 us
    all_gather x1, waiting for transfers between devices, local(): state_pool = lax.all_gather(final_states, 'group', axis=0, tiled=True)  28.3 us
  transfers between devices with their start and end apart: 2, of which 2 were waited for; matrix products, arithmetic and copies ran while one was open for 1% of the time, Pallas kernels for 0%

commit v1 on v0

v1 whole, which is shorter than its diff:
```python
import functools
import jax
import jax.numpy as jnp
from jax import lax
from jax.experimental import pallas as pl
from jax.experimental.pallas import tpu as pltpu
from jax.sharding import PartitionSpec as P

MESH = pl.DeviceIdType.MESH
F32 = jnp.float32
LOG2E = 1.4426950408889634


def softplus(v):
    return jnp.maximum(v, 0.0) + jnp.log1p(jnp.exp(-jnp.abs(v)))


def silu(v):
    return v / (1.0 + jnp.exp(-v))


def project_kernel(n, px_ref, dx_ref, w_ref, out_ref, part, recv, send_sem, recv_sem, gsend_sem, grecv_sem):
    me = lax.axis_index("tp")
    rows = part.shape[2]
    barrier = pltpu.get_barrier_semaphore()
    for k in range(1, n):
        pl.semaphore_signal(barrier, inc=1, device_id={"tp": lax.rem(me + k, n)}, device_id_type=MESH)

    def scatter(phase, k):
        peer = lax.rem(me + k, n)
        return pltpu.make_async_remote_copy(
            src_ref=part.at[phase, peer],
            dst_ref=recv.at[phase, k - 1],
            send_sem=send_sem.at[phase, k - 1],
            recv_sem=recv_sem.at[phase, k - 1],
            device_id={"tp": peer},
            device_id_type=MESH,
        )

    def gather(phase, k):
        return pltpu.make_async_remote_copy(
            src_ref=out_ref.at[phase, me],
            dst_ref=out_ref.at[phase, me],
            send_sem=gsend_sem.at[phase, k - 1],
            recv_sem=grecv_sem.at[phase, k - 1],
            device_id={"tp": lax.rem(me + k, n)},
            device_id_type=MESH,
        )

    for phase, x_ref in enumerate((px_ref, dx_ref)):
        res = jnp.dot(x_ref[...], w_ref[...], preferred_element_type=F32)
        for j in range(n):
            part[phase, j] = res[j * rows:(j + 1) * rows]
        if phase == 0:
            pl.semaphore_wait(barrier, n - 1)
        for k in range(1, n):
            scatter(phase, k).start()
    for phase in range(2):
        total = part[phase, me]
        for k in range(1, n):
            scatter(phase, k).wait_recv()
            total = total + recv[phase, k - 1]
        out_ref[phase, me] = total
        for k in range(1, n):
            gather(phase, k).start()
    for phase in range(2):
        for k in range(1, n):
            scatter(phase, k).wait_send()
            gather(phase, k).wait_send()
            source = lax.rem(me + n - k, n)
            pltpu.make_async_remote_copy(
                src_ref=out_ref.at[phase, source],
                dst_ref=out_ref.at[phase, source],
                send_sem=gsend_sem.at[phase, k - 1],
                recv_sem=grecv_sem.at[phase, k - 1],
                device_id={"tp": lax.rem(me + k, n)},
                device_id_type=MESH,
            ).wait_recv()


def project(px, dx, w, n):
    tokens, channels = px.shape
    width = w.shape[1]
    rows = tokens // n
    vmem = pl.BlockSpec(memory_space=pltpu.VMEM)
    out = pl.pallas_call(
        functools.partial(project_kernel, n),
        out_shape=jax.ShapeDtypeStruct((2, n, rows, width), F32),
        in_specs=[vmem] * 3,
        out_specs=vmem,
        scratch_shapes=[
            pltpu.VMEM((2, n, rows, width), F32),
            pltpu.VMEM((2, n - 1, rows, width), F32),
            pltpu.SemaphoreType.DMA((2, n - 1)),
            pltpu.SemaphoreType.DMA((2, n - 1)),
            pltpu.SemaphoreType.DMA((2, n - 1)),
            pltpu.SemaphoreType.DMA((2, n - 1)),
        ],
        compiler_params=pltpu.CompilerParams(
            collective_id=0, has_side_effects=True, vmem_limit_bytes=40 * 1024 * 1024
        ),
        name="project",
    )(px, dx, w)
    return out.reshape(2, tokens, width)


def step_sizes(proj, rank, w_ref, bias_ref):
    low = proj[:, :rank].astype(jnp.bfloat16)
    return softplus(jnp.dot(low, w_ref[...], preferred_element_type=F32) + bias_ref[...])


def prefill_kernel(proj_ref, x_ref, gate_ref, len_ref, w_ref, bias_ref, alog_ref, skip_ref,
                   out_ref, fin_ref, decay, force, mix, hs):
    rank = w_ref.shape[0]
    tokens, block = x_ref.shape
    states = alog_ref.shape[0]
    requests = fin_ref.shape[0]
    step = step_sizes(proj_ref[0], rank, w_ref, bias_ref)
    position = lax.broadcasted_iota(jnp.int32, (tokens, block), 0)
    first = position == 0
    ends = []
    at = jnp.int32(0)
    for k in range(requests):
        at = at + len_ref[0, k]
        ends.append(at - 1)
        if k < requests - 1:
            first = first | (position == at)
    values = x_ref[...].astype(F32)
    decay[...] = jnp.where(first, 1e30, step)
    force[...] = step * values
    rates = -jnp.exp(alog_ref[...]) * LOG2E

    def body(b, h):
        base = pl.multiple_of(b * 8, 8)
        d8 = decay[pl.ds(base, 8), :]
        f8 = force[pl.ds(base, 8), :]
        bc = proj_ref[0, pl.ds(base, 8), rank:rank + 2 * states].T
        rows = []
        for j in range(8):
            da = jnp.exp2(d8[j:j + 1] * rates)
            h = da * h + bc[:states, j:j + 1] * f8[j:j + 1]
            hs[base + j] = h
            rows.append(jnp.sum(bc[states:, j:j + 1] * h, axis=0, keepdims=True))
        mix[pl.ds(base, 8), :] = jnp.concatenate(rows, axis=0)
        return h

    lax.fori_loop(0, tokens // 8, body, jnp.zeros((states, block), F32))
    for k in range(requests):
        fin_ref[k] = hs[ends[k]]
    out_ref[...] = ((mix[...] + skip_ref[...] * values) * silu(gate_ref[...].astype(F32))).astype(out_ref.dtype)


def prefill(proj, x, gate, lengths, w, bias, alog, skip, block):
    tokens, channels = x.shape
    rank, states = w.shape[0], alog.shape[0]
    requests = lengths.shape[1]
    lane = lambda rows: pl.BlockSpec((rows, block), lambda i: (0, i))
    return pl.pallas_call(
        prefill_kernel,
        grid=(channels // block,),
        out_shape=(
            jax.ShapeDtypeStruct((tokens, channels), jnp.bfloat16),
            jax.ShapeDtypeStruct((requests, states, channels), F32),
        ),
        in_specs=[
            pl.BlockSpec((1,) + proj.shape[1:], lambda i: (0, 0, 0)),
            lane(tokens), lane(tokens),
            pl.BlockSpec(memory_space=pltpu.SMEM),
            lane(rank), lane(1), lane(states), lane(1),
        ],
        out_specs=(lane(tokens), pl.BlockSpec((requests, states, block), lambda i: (0, 0, i))),
        scratch_shapes=[
            pltpu.VMEM((tokens, block), F32),
            pltpu.VMEM((tokens, block), F32),
            pltpu.VMEM((tokens, block), F32),
            pltpu.VMEM((tokens, states, block), F32),
        ],
        compiler_params=pltpu.CompilerParams(vmem_limit_bytes=40 * 1024 * 1024),
        name="prefill",
    )(proj, x, gate, lengths, w, bias, alog, skip)


def decode_kernel(proj_ref, x_ref, gate_ref, cache_ref, pool_ref, routes_ref, w_ref, bias_ref, alog_ref, skip_ref,
                  out_ref, decay, force, mix, source):
    rank = w_ref.shape[0]
    steps, rows, block = x_ref.shape
    states = alog_ref.shape[0]
    mine = lax.axis_index("group")
    for i in range(rows):
        source[i] = 0

    def find(r, count):
        hit = routes_ref[r, 0] == mine

        @pl.when(hit)
        def _():
            source[count] = r

        return count + hit.astype(jnp.int32)

    count = lax.fori_loop(0, routes_ref.shape[0], find, jnp.int32(0))
    step = step_sizes(proj_ref[0], rank, w_ref, bias_ref)
    values = x_ref[...].astype(F32)
    decay[...] = step.reshape(steps, rows, block)
    force[...] = decay[...] * values
    rates = -jnp.exp(alog_ref[...]) * LOG2E

    def body(b, carry):
        base = pl.multiple_of(b * 8, 8)
        bcs = [proj_ref[0, pl.ds(pl.multiple_of(i * rows + base, 8), 8), rank:rank + 2 * states].T for i in range(steps)]
        outs = [[] for _ in range(steps)]
        d8 = [decay[i, pl.ds(base, 8), :] for i in range(steps)]
        f8 = [force[i, pl.ds(base, 8), :] for i in range(steps)]
        for j in range(8):
            n = base + j
            h = jnp.where(n < count, pool_ref[source[n]], cache_ref[n])
            for i in range(steps):
                da = jnp.exp2(d8[i][j:j + 1] * rates)
                h = da * h + bcs[i][:states, j:j + 1] * f8[i][j:j + 1]
                outs[i].append(jnp.sum(bcs[i][states:, j:j + 1] * h, axis=0, keepdims=True))
        for i in range(steps):
            mix[i, pl.ds(base, 8), :] = jnp.concatenate(outs[i], axis=0)
        return carry

    lax.fori_loop(0, rows // 8, body, 0)
    out_ref[...] = ((mix[...] + skip_ref[...] * values) * silu(gate_ref[...].astype(F32))).astype(out_ref.dtype)


def decode(proj, x, gate, cache, pool, routes, w, bias, alog, skip, block):
    steps, rows, channels = x.shape
    rank, states = w.shape[0], alog.shape[0]
    lane = lambda r: pl.BlockSpec((r, block), lambda i: (0, i))
    lane3 = lambda a, r: pl.BlockSpec((a, r, block), lambda i: (0, 0, i))
    return pl.pallas_call(
        decode_kernel,
        grid=(channels // block,),
        out_shape=jax.ShapeDtypeStruct((steps, rows, channels), jnp.bfloat16),
        in_specs=[
            pl.BlockSpec((1,) + proj.shape[1:], lambda i: (1, 0, 0)),
            lane3(steps, rows), lane3(steps, rows), lane3(rows, states), lane3(pool.shape[0], states),
            pl.BlockSpec(memory_space=pltpu.SMEM),
            lane(rank), lane(1), lane(states), lane(1),
        ],
        out_specs=lane3(steps, rows),
        scratch_shapes=[
            pltpu.VMEM((steps, rows, block), F32),
            pltpu.VMEM((steps, rows, block), F32),
            pltpu.VMEM((steps, rows, block), F32),
            pltpu.SMEM((rows,), jnp.int32),
        ],
        compiler_params=pltpu.CompilerParams(vmem_limit_bytes=40 * 1024 * 1024),
        name="decode",
    )(proj, x, gate, cache, pool, routes, w, bias, alog, skip)


def local(n_tp, prefill_x, prefill_gate, lengths, routes, decode_x, decode_gate, cached_state,
          xproj_weight, dt_weight, dt_bias, a_log, skip_gain):
    steps, rows, channels = decode_x.shape
    proj = project(prefill_x, decode_x.reshape(steps * rows, channels), xproj_weight, n_tp)
    bias, skip = dt_bias[None], skip_gain[None]
    out, final = prefill(proj, prefill_x, prefill_gate, lengths, dt_weight, bias, a_log, skip, min(512, channels))
    pool = lax.all_gather(final, "group", axis=0, tiled=True)
    dec = decode(proj, decode_x, decode_gate, cached_state, pool, routes, dt_weight, bias, a_log, skip, min(512, channels))
    return out, dec


def solution(mesh):
    placed = (
        P("group", "tp"),
        P("group", "tp"),
        P("group", None),
        P(),
        P(None, "group", "tp"),
        P(None, "group", "tp"),
        P("group", None, "tp"),
        P("tp", None),
        P(None, "tp"),
        P("tp"),
        P(None, "tp"),
        P("tp"),
    )
    return jax.shard_map(
        functools.partial(local, mesh.shape["tp"]),
        mesh=mesh,
        in_specs=placed,
        out_specs=(P("group", "tp"), P(None, "group", "tp")),
        check_vma=False,
    )
```

time: 1070 us -> 127 us (0.12); the launches traced: 1050 us -> 126 us
  local copies, waits for them, and re-layouts: 714 us -> 11.8 us
  other arithmetic: 200 us -> 0 us
  Pallas kernels: 0 us -> 64.2 us
  waiting for transfers between devices: 99.7 us -> 35.6 us
  matrix products: 19.2 us -> 0 us
    slice x55 -> x0, local copies, waits for them, and re-layouts: 434 us -> none  [the longest x44 432 us: local(): lax.associative_scan(combine, (damping, forcing), axis=0)]
    pad x24 -> x0, local copies, waits for them, and re-layouts: 252 us -> none  [local(): lax.associative_scan(combine, (damping, forcing), axis=0)]
    mul x13 -> x0, other arithmetic: 77.1 us -> none  [the longest x12 69.8 us: combine(): return (earlier[0] * latter[0], latter[0] * earlier[1] + latter[1])]
    psum x1 -> x0, waiting for transfers between devices: 71.4 us -> none  [local(): prefill_proj = lax.psum(prefill_part, 'tp')]
    pallas_call x0 -> x3, Pallas kernels: none -> 64.2 us  [the longest x1 33.3 us: project(): pl.pallas_call(functools.partial(project_kernel, n), out_shape=jax.ShapeD...]
    add x13 -> x0, other arithmetic: 44.1 us -> none  [the longest x12 44.1 us: local(): lax.associative_scan(combine, (damping, forcing), axis=0)]
    reduce_sum x3 -> x0, other arithmetic: 40.6 us -> none  [the longest x2 40.5 us: gated_output(): mixed = jnp.sum(readout[:, :, None] * hidden, axis=1)]
    concatenate x12 -> x0, other arithmetic: 31.1 us -> none  [local(): lax.associative_scan(combine, (damping, forcing), axis=0)]
  transfers between devices with their start and end apart: 2 -> 1, of which waited for: 2 -> 1; matrix products, arithmetic and copies ran while one was open for 1% -> 0% of each run, Pallas kernels for 0% -> 0%
where the time goes in v1:
time: 127 us; the launch traced here: 126 us
  Pallas kernels  64.2 us (51%)
  waiting for transfers between devices  35.6 us (28%)
  between operations  14.2 us (11%)
  local copies, waits for them, and re-layouts  11.8 us (9%)
    all_gather x1, waiting for transfers between devices, local(): pool = lax.all_gather(final, 'group', axis=0, tiled=True)  35.6 us
    pallas_call x1, Pallas kernels, project(): pl.pallas_call(functools.partial(project_kernel, n), out_shape=jax.ShapeD...  33.3 us
    pallas_call x1, Pallas kernels, prefill(): pl.pallas_call(prefill_kernel, grid=(channels // block,), out_shape=(jax....  17.8 us
    pallas_call x1, Pallas kernels, decode(): pl.pallas_call(decode_kernel, grid=(channels // block,), out_shape=jax.Sh...  13.1 us
    unnamed x32, local copies, waits for them, and re-layouts  11.8 us
  transfers between devices with their start and end apart: 1, of which 1 were waited for; matrix products, arithmetic and copies ran while one was open for 0% of the time, Pallas kernels for 0%

profile of v1, /device:TPU:13, one launch (start us, length us, event | category | flops | bytes accessed | tf_op | source)
XLA Modules:
  0.0 125.8 jit_solution(17091770699989269708)
XLA Ops:
  7.2 0.0 all-gather.2.cloned.1.call-start
  7.2 3.1 %copy.16.w_ref = bf16[2048,544]{1,0:T(8,128)(2,1)S(1)} copy(bf16[2048,544]{0,1:T(8,128)(2,1)} %param.19) | data formatting | bytes 4456448 | tf_op args[7]
  10.3 0.0 copy-start
  10.3 0.0 copy-start.4
  10.3 1.2 copy-done.4
  11.5 0.0 copy-start.5
  11.5 1.0 copy-done.5
  12.5 0.0 copy-start.8
  12.5 0.0 copy-start.9
  12.5 0.0 copy-start.11
  12.5 0.0 copy-start.12
  12.5 0.0 copy-start.13
  12.6 33.3 %project.1 = f32[2,8,16,544]{3,2,1,0:T(8,128)S(1)} custom-call(bf16[128,2048]{1,0:T(8,128)(2,1)S(1)} %copy-done.4, bf16[128,2048]{1,0:T(8,128)(2,1)S(1)} %bitcast.6, bf16[2048,544]{1,0:T(8,128)(2,1)S(1)} %copy.16.w_ref), custom_call_target="tpu_custom_call" | custom-call | tf_op jit(solution)/shard_map/project/pallas_call | solution.py:86
  45.9 0.0 copy-start.14
  45.9 0.0 copy-start.1
  45.9 0.0 copy-start.6
  45.9 0.0 copy-done
  45.9 0.0 copy-done.8
  45.9 0.0 copy-done.9
  46.0 0.0 copy-done.11
  46.0 0.0 copy-done.12
  46.0 0.0 copy-done.13
  46.0 17.8 %prefill.1 = (bf16[128,2048]{1,0:T(8,128)(2,1)}, f32[8,16,2048]{2,1,0:T(8,128)S(1)}) custom-call(f32[2,128,544]{2,1,0:T(8,128)S(1)} %bitcast.4, bf16[128,2048]{1,0:T(8,128)(2,1)S(1)} %copy-done.4, bf16[128,2048]{1,0:T(8,128)(2,1)S(1)} %copy-done.9, s32[1,8]{1,0:T(1,128)S(1)} %copy-done.13, bf16[512,2048]{1,0:T(8,128)(2,1)S(1)} %copy-done, ...), custom_call_target="tpu_custom_call" | custom-call | tf_op jit(solution)/shard_map/prefill/pallas_call | solution.py:158
  63.7 0.0 copy-start.7
  63.7 1.0 copy-done.7
  64.7 0.0 all-gather.2.cloned.1.call-update
  64.7 0.0 copy-done.14
  64.8 0.1 copy.17.routes_ref
  64.8 35.6 %all-gather.2.cloned.1.call-done.pool_ref = f32[32,16,2048]{2,1,0:T(8,128)} async-done(((f32[8,16,2048]{2,1,0:T(8,128)}), f32[32,16,2048]{2,1,0:T(8,128)}) %all-gather.2.cloned.1.call-update) | async-done | bytes 4194320 | tf_op jit(solution)/shard_map/all_gather | solution.py:262
  100.5 0.0 copy-done.1
  100.5 0.0 copy-done.6
  100.5 0.0 copy-start.2
  100.5 2.2 %copy-done.2 = f32[32,16,2048]{2,1,0:T(8,128)S(1)} copy-done((f32[32,16,2048]{2,1,0:T(8,128)S(1)}, f32[32,16,2048]{2,1,0:T(8,128)}, u32[]{:S(2)}) %copy-start.2) | copy-done | bytes 4194328
  102.7 0.0 copy-start.3
  102.7 2.2 %copy-done.3 = f32[32,16,2048]{2,1,0:T(8,128)S(1)} copy-done((f32[32,16,2048]{2,1,0:T(8,128)S(1)}, f32[32,16,2048]{2,1,0:T(8,128)}, u32[]{:S(2)}) %copy-start.3) | copy-done | bytes 4194328
  104.8 0.0 copy-start.10
  104.8 1.0 copy-done.10
  105.9 13.1 %decode.1 = bf16[4,32,2048]{2,1,0:T(8,128)(2,1)} custom-call(f32[2,128,544]{2,1,0:T(8,128)S(1)} %bitcast.5, bf16[4,32,2048]{2,1,0:T(8,128)(2,1)S(1)} %copy-done.6, bf16[4,32,2048]{2,1,0:T(8,128)(2,1)S(1)} %copy-done.10, f32[32,16,2048]{2,1,0:T(8,128)S(1)} %copy-done.2, f32[32,16,2048]{2,1,0:T(8,128)S(1)} %copy-done.3, s32[32,1]{1,0:T(8,128)S(1)} %copy.17.routes_ref, ...), custom_call_target="tpu_custom_call" | custom-call | tf_op jit(solution)/shard_map/decode/pallas_call | solution.py:234
Async XLA Ops:
  7.2 93.3 %all-gather.2.cloned.1.call-start = ((), (), s32[]{:S(2)}) async-start(), calls=%async_computation | async-start | bytes 5242880 | tf_op jit(solution)/shard_map/all_gather | solution.py:262
  10.3 35.6 %copy-start = (bf16[512,2048]{1,0:T(8,128)(2,1)S(1)}, bf16[512,2048]{1,0:T(8,128)(2,1)}, u32[]{:S(2)}) copy-start(bf16[512,2048]{1,0:T(8,128)(2,1)} %w_ref.4) | copy-start | bytes 6291460
  10.3 1.2 copy-start.4
  11.5 1.0 copy-start.5
  12.5 33.4 %copy-start.8 = (f32[16,2048]{1,0:T(8,128)S(1)}, f32[16,2048]{1,0:T(8,128)}, u32[]{:S(2)}) copy-start(f32[16,2048]{1,0:T(8,128)} %alog_ref.3) | copy-start | bytes 393220
  12.5 33.4 %copy-start.9 = (bf16[128,2048]{1,0:T(8,128)(2,1)S(1)}, bf16[128,2048]{1,0:T(8,128)(2,1)}, u32[]{:S(2)}) copy-start(bf16[128,2048]{1,0:T(8,128)(2,1)} %gate_ref.2) | copy-start | bytes 1572868
  12.5 33.4 %copy-start.11 = (f32[2048]{0:T(1024)S(1)}, f32[2048]{0:T(1024)}, u32[]{:S(2)}) copy-start(f32[2048]{0:T(1024)} %param.21) | copy-start | bytes 24580
  12.5 33.4 %copy-start.12 = (f32[2048]{0:T(1024)S(1)}, f32[2048]{0:T(1024)}, u32[]{:S(2)}) copy-start(f32[2048]{0:T(1024)} %param.23) | copy-start | bytes 24580
  12.5 33.4 %copy-start.13 = (s32[1,8]{1,0:T(1,128)S(1)}, s32[1,8]{1,0:T(1,128)}, u32[]{:S(2)}) copy-start(s32[1,8]{1,0:T(1,128)} %len_ref.1) | copy-start | bytes 100
  45.9 18.9 %copy-start.14 = (s32[32,1]{0,1:T(1,128)S(1)}, s32[32,1]{0,1:T(1,128)}, u32[]{:S(2)}) copy-start(s32[32,1]{0,1:T(1,128)} %param.15) | copy-start | bytes 388
  45.9 54.6 %copy-start.1 = (bf16[512,2048]{1,0:T(8,128)(2,1)S(1)}, bf16[512,2048]{1,0:T(8,128)(2,1)}, u32[]{:S(2)}) copy-start(bf16[512,2048]{1,0:T(8,128)(2,1)} %w_ref.4) | copy-start | bytes 6291460
  45.9 54.5 %copy-start.6 = (bf16[4,32,2048]{2,1,0:T(8,128)(2,1)S(1)}, bf16[4,32,2048]{2,1,0:T(8,128)(2,1)}, u32[]{:S(2)}) copy-start(bf16[4,32,2048]{2,1,0:T(8,128)(2,1)} %x_ref.3) | copy-start | bytes 1572868
  63.7 1.0 copy-start.7
  100.5 2.2 %copy-start.2 = (f32[32,16,2048]{2,1,0:T(8,128)S(1)}, f32[32,16,2048]{2,1,0:T(8,128)}, u32[]{:S(2)}) copy-start(f32[32,16,2048]{2,1,0:T(8,128)} %cache_ref.1) | copy-start | bytes 12582916
  102.7 2.2 %copy-start.3 = (f32[32,16,2048]{2,1,0:T(8,128)S(1)}, f32[32,16,2048]{2,1,0:T(8,128)}, u32[]{:S(2)}) copy-start(f32[32,16,2048]{2,1,0:T(8,128)} %all-gather.2.cloned.1.call-done.pool_ref) | copy-start | bytes 12582916
  104.8 1.0 copy-start.10
Sparse Core Ops, SparseCore 0:
  64.9 35.5 all-gather.1

commit v2 on v0

v2 whole, which is shorter than its diff:
```python
import functools
import jax
import jax.numpy as jnp
from jax import lax
from jax.experimental import pallas as pl
from jax.experimental.pallas import tpu as pltpu
from jax.sharding import PartitionSpec as P

MESH = pl.DeviceIdType.MESH
F32 = jnp.float32
BF16 = jnp.bfloat16
LOG2E = 1.4426950408889634
SET = 16


def softplus(v):
    return jnp.maximum(v, 0.0) + jnp.log1p(jnp.exp(-jnp.abs(v)))


def silu(v):
    return v / (1.0 + jnp.exp(-v))


def dot_nt(a, b):
    return lax.dot_general(a, b, (((1,), (1,)), ((), ())), preferred_element_type=F32)


def dot_tn(a, b):
    return lax.dot_general(a, b, (((0,), (0,)), ((), ())), preferred_element_type=F32)


def kernel(n, ng, cap, block, len_ref, routes_ref, px_hbm, dx_hbm, w_hbm, pg_hbm, dg_hbm, cache_hbm, dtw_hbm,
           bias_ref, alog_ref, skip_ref, outp_ref, outd_ref,
           px, dx, w, pg, dg, cache, dtw, part, recv, full, low, lhs_c, lhs_b,
           decay, force, forced, hb, hs, mix, state_out, state_in,
           in_sem, send_sem, recv_sem, gsend_sem, grecv_sem, hsend_sem, hrecv_sem):
    me = lax.axis_index("tp")
    group = lax.axis_index("group")
    tokens, channels = px.shape
    steps, rows, _ = dx.shape
    rank = dtw.shape[0]
    states = alog_ref.shape[0]
    requests = len_ref.shape[1]
    blocks = channels // block
    piece = part.shape[2]
    slots = min(ng * cap, rows)

    loads = [
        pltpu.make_async_copy(src, dst, in_sem.at[i])
        for i, (src, dst) in enumerate(
            ((w_hbm, w), (px_hbm, px), (dx_hbm, dx), (dtw_hbm, dtw), (pg_hbm, pg), (cache_hbm, cache), (dg_hbm, dg))
        )
    ]
    for load in loads:
        load.start()
    barrier = pltpu.get_barrier_semaphore()
    for k in range(1, n):
        pl.semaphore_signal(barrier, inc=1, device_id={"tp": lax.rem(me + k, n)}, device_id_type=MESH)
    for k in range(1, ng):
        pl.semaphore_signal(barrier, inc=1, device_id={"group": lax.rem(group + k, ng)}, device_id_type=MESH)

    def scatter(phase, k):
        peer = lax.rem(me + k, n)
        return pltpu.make_async_remote_copy(
            src_ref=part.at[phase, peer],
            dst_ref=recv.at[phase, k - 1],
            send_sem=send_sem.at[phase, k - 1],
            recv_sem=recv_sem.at[phase, k - 1],
            device_id={"tp": peer},
            device_id_type=MESH,
        )

    def gather(phase, k, owner):
        return pltpu.make_async_remote_copy(
            src_ref=full.at[phase, owner],
            dst_ref=full.at[phase, owner],
            send_sem=gsend_sem.at[phase, k - 1],
            recv_sem=grecv_sem.at[phase, k - 1],
            device_id={"tp": lax.rem(me + k, n)},
            device_id_type=MESH,
        )

    def handoff(b, k):
        return pltpu.make_async_remote_copy(
            src_ref=state_out.at[b, k - 1],
            dst_ref=state_in.at[b, k],
            send_sem=hsend_sem.at[b, k - 1],
            recv_sem=hrecv_sem.at[b, k - 1],
            device_id={"group": lax.rem(group + k, ng)},
            device_id_type=MESH,
        )

    for phase in range(2):
        if phase == 0:
            loads[0].wait()
            loads[1].wait()
            values = px[...]
        else:
            loads[2].wait()
            values = dx[...].reshape(steps * rows, channels)
        res = dot_nt(w[...], values)
        for j in range(n):
            part[phase, j] = res[j * piece:(j + 1) * piece]
        if phase == 0:
            pl.semaphore_wait(barrier, n - 1 + ng - 1)
        for k in range(1, n):
            scatter(phase, k).start()

    ends = []
    at = jnp.int32(0)
    for k in range(requests):
        at = at + len_ref[0, k]
        ends.append(at)
    leaving = []
    for k in range(ng):
        dest = lax.rem(group + k, ng)
        found = [jnp.int32(0)] * cap
        count = jnp.int32(0)
        for q in range(requests):
            hit = routes_ref[group * requests + q, 0] == dest
            found = [jnp.where(hit & (count == r), jnp.maximum(ends[q] - 1, 0), found[r]) for r in range(cap)]
            count = count + hit.astype(jnp.int32)
        leaving.append(found)

    def locate(origin, carry):
        count, places = carry[0], list(carry[1:])
        arrived = jnp.int32(0)
        turn = lax.rem(group + ng - origin, ng)
        for q in range(requests):
            hit = routes_ref[origin * requests + q, 0] == group
            places = [jnp.where(hit & (count == r), turn * cap + arrived, places[r]) for r in range(slots)]
            count = count + hit.astype(jnp.int32)
            arrived = arrived + hit.astype(jnp.int32)
        return (count, *places)

    located = lax.fori_loop(0, ng, locate, (jnp.int32(0),) * (slots + 1))
    taken, places = located[0], located[1:]

    for phase in range(2):
        total = part[phase, me]
        for k in range(1, n):
            scatter(phase, k).wait_recv()
            total = total + recv[phase, k - 1]
        full[phase, me] = total
        for k in range(1, n):
            gather(phase, k, me).start()

    tile = (lax.broadcasted_iota(jnp.int32, (states, SET * states), 1) % states
            == lax.broadcasted_iota(jnp.int32, (states, SET * states), 0)).astype(F32)

    def collect(phase):
        for k in range(1, n):
            gather(phase, k, lax.rem(me + n - k, n)).wait_recv()
        proj = jnp.concatenate([full[phase, j] for j in range(n)], axis=0)
        low[phase] = proj[:rank].astype(BF16)
        width = proj.shape[1]
        spread_b = dot_tn(tile, proj[rank:rank + states])
        own = (lax.broadcasted_iota(jnp.int32, (SET * states, width), 0) // states
               == lax.broadcasted_iota(jnp.int32, (SET * states, width), 1) % SET)
        spread_b = jnp.where(own, spread_b, 0.0).astype(BF16)
        spread_c = dot_tn(proj[rank + states:], tile)
        own = (lax.broadcasted_iota(jnp.int32, (width, SET * states), 1) // states
               == lax.broadcasted_iota(jnp.int32, (width, SET * states), 0) % SET)
        lhs_c[phase] = jnp.where(own, spread_c, 0.0).astype(BF16)
        for s in range(width // SET):
            lhs_b[phase, s] = spread_b[:, s * SET:(s + 1) * SET]

    def step_sizes(phase, lanes):
        return softplus(dot_tn(low[phase], dtw[:, lanes]) + bias_ref[:, lanes])

    collect(0)
    loads[3].wait()
    loads[4].wait()
    position = lax.broadcasted_iota(jnp.int32, (tokens, block), 0)
    first = position == 0
    for k in range(requests - 1):
        first = first | (position == ends[k])

    def prefill_block(b, carry):
        lanes = pl.ds(pl.multiple_of(b * block, block), block)
        step = step_sizes(0, lanes)
        values = px[:, lanes].astype(F32)
        decay[...] = jnp.where(first, 1e30, step)
        force[...] = (step * values).astype(BF16)
        rates = -jnp.exp(alog_ref[:, lanes]) * LOG2E

        def some(s, h):
            base = pl.multiple_of(s * SET, SET)
            forced[0] = jnp.dot(lhs_b[0, s], force[pl.ds(base, SET), :], preferred_element_type=F32)
            for j in range(SET):
                da = jnp.exp2(decay[pl.ds(base + j, 1), :] * rates)
                h = da * h + forced[0, j * states:(j + 1) * states, :]
                hs[base + j] = h
                hb[0, j * states:(j + 1) * states, :] = h.astype(BF16)
            mix[pl.ds(base, SET), :] = jnp.dot(lhs_c[0, pl.ds(base, SET), :], hb[0], preferred_element_type=F32)
            return h

        lax.fori_loop(0, tokens // SET, some, jnp.zeros((states, block), F32))
        for k in range(1, ng):
            for r in range(cap):
                state_out[b, k - 1, r] = hs[leaving[k][r]]
            handoff(b, k).start()
        for r in range(cap):
            state_in[b, 0, r] = hs[leaving[0][r]]
        outp_ref[:, lanes] = ((mix[...] + skip_ref[:, lanes] * values) * silu(pg[:, lanes].astype(F32))).astype(BF16)
        return carry

    lax.fori_loop(0, blocks, prefill_block, 0)

    collect(1)
    loads[5].wait()
    loads[6].wait()

    def decode_rows(b, base, takes):
        lanes = pl.ds(pl.multiple_of(b * block, block), block)
        step = step_sizes(1, lanes).reshape(steps, rows, block)[:, base:base + SET]
        values = dx[:, base:base + SET, lanes].astype(F32)
        now = pl.ds(0, SET)
        for i in range(steps):
            decay[i * SET:(i + 1) * SET, :] = step[i]
            forced[i] = jnp.dot(lhs_b[1, (i * rows + base) // SET], (step[i] * values[i]).astype(BF16),
                                preferred_element_type=F32)
        rates = -jnp.exp(alog_ref[:, lanes]) * LOG2E
        for j in range(SET):
            row = base + j
            h = cache[row, :, lanes]
            if takes and row < slots:
                place = places[row]
                h = jnp.where(row < taken, hs[place], h)
            for i in range(steps):
                da = jnp.exp2(decay[i * SET + j:i * SET + j + 1, :] * rates)
                h = da * h + forced[i, j * states:(j + 1) * states, :]
                hb[i, j * states:(j + 1) * states, :] = h.astype(BF16)
        skip = skip_ref[:, lanes]
        for i in range(steps):
            at = i * rows + base
            mixed = jnp.dot(lhs_c[1, at:at + SET, :], hb[i], preferred_element_type=F32)
            gate = silu(dg[i, base:base + SET, lanes].astype(F32))
            outd_ref[i, base:base + SET, lanes] = ((mixed + skip * values[i]) * gate).astype(BF16)

    late = [base for base in range(0, rows, SET) if base < slots]
    early = [base for base in range(0, rows, SET) if base >= slots]

    def early_block(b, carry):
        for base in early:
            decode_rows(b, base, False)
        return carry

    def late_block(b, carry):
        for k in range(1, ng):
            handoff(b, k).wait_recv()
        for k in range(ng):
            for r in range(cap):
                hs[k * cap + r] = state_in[b, k, r]
        for base in late:
            decode_rows(b, base, True)
        return carry

    lax.fori_loop(0, blocks, early_block, 0)
    lax.fori_loop(0, blocks, late_block, 0)

    for phase in range(2):
        for k in range(1, n):
            scatter(phase, k).wait_send()
            gather(phase, k, me).wait_send()

    def finish(b, carry):
        for k in range(1, ng):
            handoff(b, k).wait_send()
        return carry

    lax.fori_loop(0, blocks, finish, 0)


def local(n, ng, prefill_x, prefill_gate, lengths, routes, decode_x, decode_gate, cached_state,
          xproj_weight, dt_weight, dt_bias, a_log, skip_gain):
    tokens, channels = prefill_x.shape
    steps, rows, _ = decode_x.shape
    rank, states = dt_weight.shape[0], a_log.shape[0]
    width = xproj_weight.shape[1]
    cap = max(1, 2 * lengths.shape[1] // ng)
    block = min(512, channels)
    blocks = channels // block
    piece = width // n
    columns = max(tokens, steps * rows)
    anywhere = pl.BlockSpec(memory_space=pl.ANY)
    smem = pl.BlockSpec(memory_space=pltpu.SMEM)
    vmem = pl.BlockSpec(memory_space=pltpu.VMEM)
    dma = pltpu.SemaphoreType.DMA
    return pl.pallas_call(
        functools.partial(kernel, n, ng, cap, block),
        out_shape=(
            jax.ShapeDtypeStruct(prefill_x.shape, BF16),
            jax.ShapeDtypeStruct(decode_x.shape, BF16),
        ),
        in_specs=[smem, smem] + [anywhere] * 7 + [vmem] * 3,
        out_specs=(vmem, vmem),
        scratch_shapes=[
            pltpu.VMEM(prefill_x.shape, BF16),
            pltpu.VMEM(decode_x.shape, BF16),
            pltpu.VMEM((width, channels), BF16),
            pltpu.VMEM(prefill_x.shape, BF16),
            pltpu.VMEM(decode_x.shape, BF16),
            pltpu.VMEM(cached_state.shape, F32),
            pltpu.VMEM(dt_weight.shape, BF16),
            pltpu.VMEM((2, n, piece, columns), F32),
            pltpu.VMEM((2, n - 1, piece, columns), F32),
            pltpu.VMEM((2, n, piece, columns), F32),
            pltpu.VMEM((2, rank, columns), BF16),
            pltpu.VMEM((2, columns, SET * states), BF16),
            pltpu.VMEM((2, columns // SET, SET * states, SET), BF16),
            pltpu.VMEM((columns, block), F32),
            pltpu.VMEM((columns, block), BF16),
            pltpu.VMEM((steps, SET * states, block), F32),
            pltpu.VMEM((steps, SET * states, block), BF16),
            pltpu.VMEM((tokens, states, block), F32),
            pltpu.VMEM((tokens, block), F32),
            pltpu.VMEM((blocks, ng - 1, cap, states, block), F32),
            pltpu.VMEM((blocks, ng, cap, states, block), F32),
            dma((7,)),
            dma((2, n - 1)),
            dma((2, n - 1)),
            dma((2, n - 1)),
            dma((2, n - 1)),
            dma((blocks, ng - 1)),
            dma((blocks, ng - 1)),
        ],
        compiler_params=pltpu.CompilerParams(
            collective_id=0, has_side_effects=True, vmem_limit_bytes=52 * 1024 * 1024
        ),
        name="layer",
    )(lengths, routes, prefill_x, decode_x, xproj_weight.T, prefill_gate, decode_gate, cached_state, dt_weight,
      dt_bias[None], a_log, skip_gain[None])


def solution(mesh):
    placed = (
        P("group", "tp"),
        P("group", "tp"),
        P("group", None),
        P(),
        P(None, "group", "tp"),
        P(None, "group", "tp"),
        P("group", None, "tp"),
        P("tp", None),
        P(None, "tp"),
        P("tp"),
        P(None, "tp"),
        P("tp"),
    )
    return jax.shard_map(
        functools.partial(local, mesh.shape["tp"], mesh.shape["group"]),
        mesh=mesh,
        in_specs=placed,
        out_specs=(P("group", "tp"), P(None, "group", "tp")),
        check_vma=False,
    )
```

time: 1070 us -> 62.4 us (0.06); the launches traced: 1050 us -> 61.8 us
  local copies, waits for them, and re-layouts: 714 us -> 6.32 us
  other arithmetic: 200 us -> 0 us
  waiting for transfers between devices: 99.7 us -> 0 us
  Pallas kernels: 0 us -> 54.9 us
  matrix products: 19.2 us -> 0 us
  between operations: 14.8 us -> 0.64 us
    slice x55 -> x0, local copies, waits for them, and re-layouts: 434 us -> none  [the longest x44 432 us: local(): lax.associative_scan(combine, (damping, forcing), axis=0)]
    pad x24 -> x0, local copies, waits for them, and re-layouts: 252 us -> none  [local(): lax.associative_scan(combine, (damping, forcing), axis=0)]
    mul x13 -> x0, other arithmetic: 77.1 us -> none  [the longest x12 69.8 us: combine(): return (earlier[0] * latter[0], latter[0] * earlier[1] + latter[1])]
    psum x1 -> x0, waiting for transfers between devices: 71.4 us -> none  [local(): prefill_proj = lax.psum(prefill_part, 'tp')]
    pallas_call x0 -> x1, Pallas kernels: none -> 54.9 us  [local(): pl.pallas_call(functools.partial(kernel, n, ng, cap, block), out_shape=(j...]
    add x13 -> x0, other arithmetic: 44.1 us -> none  [the longest x12 44.1 us: local(): lax.associative_scan(combine, (damping, forcing), axis=0)]
    reduce_sum x3 -> x0, other arithmetic: 40.6 us -> none  [the longest x2 40.5 us: gated_output(): mixed = jnp.sum(readout[:, :, None] * hidden, axis=1)]
    concatenate x12 -> x0, other arithmetic: 31.1 us -> none  [local(): lax.associative_scan(combine, (damping, forcing), axis=0)]
  transfers between devices with their start and end apart: 2 -> 0, of which waited for: 2 -> 0; matrix products, arithmetic and copies ran while one was open for 1% -> 0% of each run, Pallas kernels for 0% -> 0%
where the time goes in v2:
time: 62.4 us; the launch traced here: 61.8 us
  Pallas kernels  54.9 us (88%)
  local copies, waits for them, and re-layouts  6.32 us (10%)
  between operations  0.64 us (1%)
    pallas_call x1, Pallas kernels, local(): pl.pallas_call(functools.partial(kernel, n, ng, cap, block), out_shape=(j...  54.9 us
    unnamed x13, local copies, waits for them, and re-layouts  6.32 us

profile of v2, /device:TPU:13, one launch (start us, length us, event | category | flops | bytes accessed | tf_op | source)
XLA Modules:
  0.0 61.8 jit_solution(8171871917755656369)
XLA Ops:
  0.6 0.7 %copy.14.routes_ref = s32[32,1]{1,0:T(8,128)S(1)} copy(s32[32,1]{0,1:T(1,128)} %param.15) | data formatting | bytes 256 | tf_op args[3]
  1.4 0.0 copy-start
  1.4 1.0 %copy-done = bf16[128,2048]{1,0:T(8,128)(2,1)S(1)} copy-done((bf16[128,2048]{1,0:T(8,128)(2,1)S(1)}, bf16[128,2048]{1,0:T(8,128)(2,1)}, u32[]{:S(2)}) %copy-start) | copy-done | bytes 524312
  2.4 0.0 copy-start.1
  2.4 0.9 %copy-done.1 = f32[16,2048]{1,0:T(8,128)S(1)} copy-done((f32[16,2048]{1,0:T(8,128)S(1)}, f32[16,2048]{1,0:T(8,128)}, u32[]{:S(2)}) %copy-start.1) | copy-done | bytes 131096
  3.3 0.0 copy-start.2
  3.3 0.7 %copy-done.2 = f32[2048]{0:T(1024)S(1)} copy-done((f32[2048]{0:T(1024)S(1)}, f32[2048]{0:T(1024)}, u32[]{:S(2)}) %copy-start.2) | copy-done | bytes 8216
  4.0 0.0 copy-start.3
  4.0 0.7 %copy-done.3 = f32[2048]{0:T(1024)S(1)} copy-done((f32[2048]{0:T(1024)S(1)}, f32[2048]{0:T(1024)}, u32[]{:S(2)}) %copy-start.3) | copy-done | bytes 8216
  4.7 0.0 copy-start.4
  4.7 0.7 %copy-done.4 = s32[1,8]{1,0:T(1,128)S(1)} copy-done((s32[1,8]{1,0:T(1,128)S(1)}, s32[1,8]{1,0:T(1,128)}, u32[]{:S(2)}) %copy-start.4) | copy-done | bytes 56
  5.4 54.9 %layer.1 = (bf16[128,2048]{1,0:T(8,128)(2,1)S(1)}, bf16[4,32,2048]{2,1,0:T(8,128)(2,1)S(1)}) custom-call(s32[1,8]{1,0:T(1,128)S(1)} %copy-done.4, s32[32,1]{1,0:T(8,128)S(1)} %copy.14.routes_ref, bf16[128,2048]{1,0:T(8,128)(2,1)S(1)} %copy-done, bf16[4,32,2048]{2,1,0:T(8,128)(2,1)} %dx_hbm.1, bf16[544,2048]{1,0:T(8,128)(2,1)} %bitcast.5, ...), custom_call_target="tpu_custom_call" | custom-call | tf_op jit(solution)/shard_map/layer/pallas_call | solution.py:290
  60.2 0.8 %copy.17 = bf16[128,2048]{1,0:T(8,128)(2,1)} copy(bf16[128,2048]{1,0:T(8,128)(2,1)S(1)} %get-tuple-element.4) | data formatting | bytes 1048576
  61.0 0.8 %copy.18 = bf16[4,32,2048]{2,1,0:T(8,128)(2,1)} copy(bf16[4,32,2048]{2,1,0:T(8,128)(2,1)S(1)} %get-tuple-element.5) | data formatting | bytes 1048576
Async XLA Ops:
  1.4 1.0 %copy-start = (bf16[128,2048]{1,0:T(8,128)(2,1)S(1)}, bf16[128,2048]{1,0:T(8,128)(2,1)}, u32[]{:S(2)}) copy-start(bf16[128,2048]{1,0:T(8,128)(2,1)} %px_hbm.1) | copy-start | bytes 1572868
  2.4 0.9 %copy-start.1 = (f32[16,2048]{1,0:T(8,128)S(1)}, f32[16,2048]{1,0:T(8,128)}, u32[]{:S(2)}) copy-start(f32[16,2048]{1,0:T(8,128)} %alog_ref.1) | copy-start | bytes 393220
  3.3 0.7 %copy-start.2 = (f32[2048]{0:T(1024)S(1)}, f32[2048]{0:T(1024)}, u32[]{:S(2)}) copy-start(f32[2048]{0:T(1024)} %param.21) | copy-start | bytes 24580
  4.0 0.7 %copy-start.3 = (f32[2048]{0:T(1024)S(1)}, f32[2048]{0:T(1024)}, u32[]{:S(2)}) copy-start(f32[2048]{0:T(1024)} %param.23) | copy-start | bytes 24580
  4.7 0.7 %copy-start.4 = (s32[1,8]{1,0:T(1,128)S(1)}, s32[1,8]{1,0:T(1,128)}, u32[]{:S(2)}) copy-start(s32[1,8]{1,0:T(1,128)} %len_ref.1) | copy-start | bytes 100

commit v3 on v2

--- a/solution.py
+++ b/solution.py
@@ -29,10 +29,16 @@
     return lax.dot_general(a, b, (((0,), (0,)), ((), ())), preferred_element_type=F32)
 
 
-def kernel(n, ng, cap, block, len_ref, routes_ref, px_hbm, dx_hbm, w_hbm, pg_hbm, dg_hbm, cache_hbm, dtw_hbm,
-           bias_ref, alog_ref, skip_ref, outp_ref, outd_ref,
+def halves(v):
+    high = v.astype(BF16)
+    return high, (v - high.astype(F32)).astype(BF16)
+
+
+def kernel(n, ng, cap, block, len_hbm, routes_hbm, px_hbm, dx_hbm, w_hbm, pg_hbm, dg_hbm, cache_hbm, dtw_hbm,
+           bias_hbm, alog_hbm, skip_hbm, outp_ref, outd_ref,
+           len_ref, routes_ref, bias_ref, alog_ref, skip_ref,
            px, dx, w, pg, dg, cache, dtw, part, recv, full, low, lhs_c, lhs_b,
-           decay, force, forced, hb, hs, mix, state_out, state_in,
+           decay, force, forced, hb, hd, mix, state_out, state_in, pool,
            in_sem, send_sem, recv_sem, gsend_sem, grecv_sem, hsend_sem, hrecv_sem):
     me = lax.axis_index("tp")
     group = lax.axis_index("group")
@@ -48,7 +54,9 @@
     loads = [
         pltpu.make_async_copy(src, dst, in_sem.at[i])
         for i, (src, dst) in enumerate(
-            ((w_hbm, w), (px_hbm, px), (dx_hbm, dx), (dtw_hbm, dtw), (pg_hbm, pg), (cache_hbm, cache), (dg_hbm, dg))
+            ((w_hbm, w), (px_hbm, px), (dx_hbm, dx), (dtw_hbm, dtw), (pg_hbm, pg), (cache_hbm, cache), (dg_hbm, dg),
+             (len_hbm, len_ref), (routes_hbm, routes_ref), (bias_hbm, bias_ref), (alog_hbm, alog_ref),
+             (skip_hbm, skip_ref))
         )
     ]
     for load in loads:
@@ -103,8 +111,10 @@
             part[phase, j] = res[j * piece:(j + 1) * piece]
         if phase == 0:
             pl.semaphore_wait(barrier, n - 1 + ng - 1)
-        for k in range(1, n):
-            scatter(phase, k).start()
+            for k in range(1, n):
+                scatter(phase, k).start()
+    for i in range(7, 12):
+        loads[i].wait()
 
     ends = []
     at = jnp.int32(0)
@@ -117,7 +127,7 @@
         found = [jnp.int32(0)] * cap
         count = jnp.int32(0)
         for q in range(requests):
-            hit = routes_ref[group * requests + q, 0] == dest
+            hit = routes_ref[0, group * requests + q] == dest
             found = [jnp.where(hit & (count == r), jnp.maximum(ends[q] - 1, 0), found[r]) for r in range(cap)]
             count = count + hit.astype(jnp.int32)
         leaving.append(found)
@@ -127,7 +137,7 @@
         arrived = jnp.int32(0)
         turn = lax.rem(group + ng - origin, ng)
         for q in range(requests):
-            hit = routes_ref[origin * requests + q, 0] == group
+            hit = routes_ref[0, origin * requests + q] == group
             places = [jnp.where(hit & (count == r), turn * cap + arrived, places[r]) for r in range(slots)]
             count = count + hit.astype(jnp.int32)
             arrived = arrived + hit.astype(jnp.int32)
@@ -136,7 +146,7 @@
     located = lax.fori_loop(0, ng, locate, (jnp.int32(0),) * (slots + 1))
     taken, places = located[0], located[1:]
 
-    for phase in range(2):
+    def reduce(phase):
         total = part[phase, me]
         for k in range(1, n):
             scatter(phase, k).wait_recv()
@@ -145,8 +155,12 @@
         for k in range(1, n):
             gather(phase, k, me).start()
 
+    reduce(0)
+    for k in range(1, n):
+        scatter(1, k).start()
+
     tile = (lax.broadcasted_iota(jnp.int32, (states, SET * states), 1) % states
-            == lax.broadcasted_iota(jnp.int32, (states, SET * states), 0)).astype(F32)
+            == lax.broadcasted_iota(jnp.int32, (states, SET * states), 0)).astype(BF16)
 
     def collect(phase):
         for k in range(1, n):
@@ -154,16 +168,25 @@
         proj = jnp.concatenate([full[phase, j] for j in range(n)], axis=0)
         low[phase] = proj[:rank].astype(BF16)
         width = proj.shape[1]
-        spread_b = dot_tn(tile, proj[rank:rank + states])
         own = (lax.broadcasted_iota(jnp.int32, (SET * states, width), 0) // states
                == lax.broadcasted_iota(jnp.int32, (SET * states, width), 1) % SET)
-        spread_b = jnp.where(own, spread_b, 0.0).astype(BF16)
-        spread_c = dot_tn(proj[rank + states:], tile)
+        high, rest = [jnp.where(own, dot_tn(tile, v), 0.0).astype(BF16) for v in halves(proj[rank:rank + states])]
+        for s in range(width // SET):
+            lhs_b[phase, s] = jnp.concatenate([v[:, s * SET:(s + 1) * SET] for v in (high, rest, high)], axis=1)
         own = (lax.broadcasted_iota(jnp.int32, (width, SET * states), 1) // states
                == lax.broadcasted_iota(jnp.int32, (width, SET * states), 0) % SET)
-        lhs_c[phase] = jnp.where(own, spread_c, 0.0).astype(BF16)
+        high, rest = [jnp.where(own, dot_tn(v, tile), 0.0).astype(BF16) for v in halves(proj[rank + states:])]
         for s in range(width // SET):
-            lhs_b[phase, s] = spread_b[:, s * SET:(s + 1) * SET]
+            lhs_c[phase, s, :SET] = high[s * SET:(s + 1) * SET]
+            lhs_c[phase, s, SET:] = rest[s * SET:(s + 1) * SET]
+
+    def forcing(phase, s, values):
+        high, rest = halves(values)
+        return jnp.dot(lhs_b[phase, s], jnp.concatenate([high, high, rest], axis=0), preferred_element_type=F32)
+
+    def readout(phase, s, hidden):
+        both = jnp.dot(lhs_c[phase, s], hidden.reshape(SET * states, block), preferred_element_type=F32)
+        return both[:SET] + both[SET:]
 
     def step_sizes(phase, lanes):
         return softplus(dot_tn(low[phase], dtw[:, lanes]) + bias_ref[:, lanes])
@@ -181,31 +204,32 @@
         step = step_sizes(0, lanes)
         values = px[:, lanes].astype(F32)
         decay[...] = jnp.where(first, 1e30, step)
-        force[...] = (step * values).astype(BF16)
+        force[...] = step * values
         rates = -jnp.exp(alog_ref[:, lanes]) * LOG2E
 
         def some(s, h):
             base = pl.multiple_of(s * SET, SET)
-            forced[0] = jnp.dot(lhs_b[0, s], force[pl.ds(base, SET), :], preferred_element_type=F32)
+            forced[0] = forcing(0, s, force[pl.ds(base, SET), :])
             for j in range(SET):
                 da = jnp.exp2(decay[pl.ds(base + j, 1), :] * rates)
                 h = da * h + forced[0, j * states:(j + 1) * states, :]
-                hs[base + j] = h
-                hb[0, j * states:(j + 1) * states, :] = h.astype(BF16)
-            mix[pl.ds(base, SET), :] = jnp.dot(lhs_c[0, pl.ds(base, SET), :], hb[0], preferred_element_type=F32)
+                hb[base + j] = h.astype(BF16)
+            mix[pl.ds(base, SET), :] = readout(0, s, hb[pl.ds(base, SET)])
             return h
 
         lax.fori_loop(0, tokens // SET, some, jnp.zeros((states, block), F32))
         for k in range(1, ng):
             for r in range(cap):
-                state_out[b, k - 1, r] = hs[leaving[k][r]]
+                state_out[b, k - 1, r] = hb[leaving[k][r]].astype(F32)
             handoff(b, k).start()
         for r in range(cap):
-            state_in[b, 0, r] = hs[leaving[0][r]]
+            state_in[b, 0, r] = hb[leaving[0][r]].astype(F32)
         outp_ref[:, lanes] = ((mix[...] + skip_ref[:, lanes] * values) * silu(pg[:, lanes].astype(F32))).astype(BF16)
         return carry
 
-    lax.fori_loop(0, blocks, prefill_block, 0)
+    lax.fori_loop(0, blocks // 2, prefill_block, 0)
+    reduce(1)
+    lax.fori_loop(blocks // 2, blocks, prefill_block, 0)
 
     collect(1)
     loads[5].wait()
@@ -218,23 +242,21 @@
         now = pl.ds(0, SET)
         for i in range(steps):
             decay[i * SET:(i + 1) * SET, :] = step[i]
-            forced[i] = jnp.dot(lhs_b[1, (i * rows + base) // SET], (step[i] * values[i]).astype(BF16),
-                                preferred_element_type=F32)
+            forced[i] = forcing(1, (i * rows + base) // SET, step[i] * values[i])
         rates = -jnp.exp(alog_ref[:, lanes]) * LOG2E
         for j in range(SET):
             row = base + j
             h = cache[row, :, lanes]
             if takes and row < slots:
                 place = places[row]
-                h = jnp.where(row < taken, hs[place], h)
+                h = jnp.where(row < taken, pool[place], h)
             for i in range(steps):
                 da = jnp.exp2(decay[i * SET + j:i * SET + j + 1, :] * rates)
                 h = da * h + forced[i, j * states:(j + 1) * states, :]
-                hb[i, j * states:(j + 1) * states, :] = h.astype(BF16)
+                hd[i, j] = h.astype(BF16)
         skip = skip_ref[:, lanes]
         for i in range(steps):
-            at = i * rows + base
-            mixed = jnp.dot(lhs_c[1, at:at + SET, :], hb[i], preferred_element_type=F32)
+            mixed = readout(1, (i * rows + base) // SET, hd[i])
             gate = silu(dg[i, base:base + SET, lanes].astype(F32))
             outd_ref[i, base:base + SET, lanes] = ((mixed + skip * values[i]) * gate).astype(BF16)
 
@@ -251,7 +273,7 @@
             handoff(b, k).wait_recv()
         for k in range(ng):
             for r in range(cap):
-                hs[k * cap + r] = state_in[b, k, r]
+                pool[k * cap + r] = state_in[b, k, r]
         for base in late:
             decode_rows(b, base, True)
         return carry
@@ -283,8 +305,7 @@
     blocks = channels // block
     piece = width // n
     columns = max(tokens, steps * rows)
-    anywhere = pl.BlockSpec(memory_space=pl.ANY)
-    smem = pl.BlockSpec(memory_space=pltpu.SMEM)
+    anywhere = pl.BlockSpec(memory_space=pltpu.HBM)
     vmem = pl.BlockSpec(memory_space=pltpu.VMEM)
     dma = pltpu.SemaphoreType.DMA
     return pl.pallas_call(
@@ -293,9 +314,14 @@
             jax.ShapeDtypeStruct(prefill_x.shape, BF16),
             jax.ShapeDtypeStruct(decode_x.shape, BF16),
         ),
-        in_specs=[smem, smem] + [anywhere] * 7 + [vmem] * 3,
+        in_specs=[anywhere] * 12,
         out_specs=(vmem, vmem),
         scratch_shapes=[
+            pltpu.SMEM(lengths.shape, jnp.int32),
+            pltpu.SMEM((1, routes.shape[0]), jnp.int32),
+            pltpu.VMEM((1, channels), F32),
+            pltpu.VMEM(a_log.shape, F32),
+            pltpu.VMEM((1, channels), F32),
             pltpu.VMEM(prefill_x.shape, BF16),
             pltpu.VMEM(decode_x.shape, BF16),
             pltpu.VMEM((width, channels), BF16),
@@ -307,17 +333,18 @@
             pltpu.VMEM((2, n - 1, piece, columns), F32),
             pltpu.VMEM((2, n, piece, columns), F32),
             pltpu.VMEM((2, rank, columns), BF16),
-            pltpu.VMEM((2, columns, SET * states), BF16),
-            pltpu.VMEM((2, columns // SET, SET * states, SET), BF16),
+            pltpu.VMEM((2, columns // SET, 2 * SET, SET * states), BF16),
+            pltpu.VMEM((2, columns // SET, SET * states, 3 * SET), BF16),
             pltpu.VMEM((columns, block), F32),
-            pltpu.VMEM((columns, block), BF16),
+            pltpu.VMEM((columns, block), F32),
             pltpu.VMEM((steps, SET * states, block), F32),
-            pltpu.VMEM((steps, SET * states, block), BF16),
-            pltpu.VMEM((tokens, states, block), F32),
+            pltpu.VMEM((tokens, states, block), BF16),
+            pltpu.VMEM((steps, SET, states, block), BF16),
             pltpu.VMEM((tokens, block), F32),
             pltpu.VMEM((blocks, ng - 1, cap, states, block), F32),
             pltpu.VMEM((blocks, ng, cap, states, block), F32),
-            dma((7,)),
+            pltpu.VMEM((ng * cap + lengths.shape[1], states, block), F32),
+            dma((12,)),
             dma((2, n - 1)),
             dma((2, n - 1)),
             dma((2, n - 1)),
@@ -329,7 +356,7 @@
             collective_id=0, has_side_effects=True, vmem_limit_bytes=52 * 1024 * 1024
         ),
         name="layer",
-    )(lengths, routes, prefill_x, decode_x, xproj_weight.T, prefill_gate, decode_gate, cached_state, dt_weight,
+    )(lengths, routes.T, prefill_x, decode_x, xproj_weight.T, prefill_gate, decode_gate, cached_state, dt_weight,
       dt_bias[None], a_log, skip_gain[None])
 
 

time: 62.4 us -> 55.8 us (0.89)
  Pallas kernels: 54.9 us -> 48.6 us
    pallas_call x1, Pallas kernels: 54.9 us -> 48.6 us  [local(): pl.pallas_call(functools.partial(kernel, n, ng, cap, block), out_shape=(j...]
    unnamed x13 -> x14, local copies, waits for them, and re-layouts: 6.32 us -> 6.23 us
where the time goes in v3:
time: 55.8 us; the launch traced here: 55.5 us
  Pallas kernels  48.6 us (87%)
  local copies, waits for them, and re-layouts  6.23 us (11%)
  between operations  0.66 us (1%)
    pallas_call x1, Pallas kernels, local(): pl.pallas_call(functools.partial(kernel, n, ng, cap, block), out_shape=(j...  48.6 us
    unnamed x14, local copies, waits for them, and re-layouts  6.23 us

profile of v3, /device:TPU:13, one launch (start us, length us, event | category | flops | bytes accessed | tf_op | source)
XLA Modules:
  0.0 55.5 jit_solution(7023484991736075722)
XLA Ops:
  0.6 0.0 copy-start
  0.6 1.0 %copy-done = bf16[128,2048]{1,0:T(8,128)(2,1)S(1)} copy-done((bf16[128,2048]{1,0:T(8,128)(2,1)S(1)}, bf16[128,2048]{1,0:T(8,128)(2,1)}, u32[]{:S(2)}) %copy-start) | copy-done | bytes 524312
  1.7 0.0 copy-start.1
  1.7 0.9 %copy-done.1 = f32[16,2048]{1,0:T(8,128)S(1)} copy-done((f32[16,2048]{1,0:T(8,128)S(1)}, f32[16,2048]{1,0:T(8,128)}, u32[]{:S(2)}) %copy-start.1) | copy-done | bytes 131096
  2.6 0.0 copy-start.2
  2.6 0.7 %copy-done.2 = f32[2048]{0:T(1024)S(1)} copy-done((f32[2048]{0:T(1024)S(1)}, f32[2048]{0:T(1024)}, u32[]{:S(2)}) %copy-start.2) | copy-done | bytes 8216
  3.3 0.0 copy-start.3
  3.3 0.7 %copy-done.3 = f32[2048]{0:T(1024)S(1)} copy-done((f32[2048]{0:T(1024)S(1)}, f32[2048]{0:T(1024)}, u32[]{:S(2)}) %copy-start.3) | copy-done | bytes 8216
  4.0 0.0 copy-start.4
  4.0 0.7 %copy-done.4 = s32[1,8]{1,0:T(1,128)S(1)} copy-done((s32[1,8]{1,0:T(1,128)S(1)}, s32[1,8]{1,0:T(1,128)}, u32[]{:S(2)}) %copy-start.4) | copy-done | bytes 56
  4.6 0.0 copy-start.5
  4.6 0.7 %copy-done.5 = s32[32,1]{0,1:T(1,128)S(1)} copy-done((s32[32,1]{0,1:T(1,128)S(1)}, s32[32,1]{0,1:T(1,128)}, u32[]{:S(2)}) %copy-start.5) | copy-done | bytes 152
  5.3 48.6 %layer.1 = (bf16[128,2048]{1,0:T(8,128)(2,1)S(1)}, bf16[4,32,2048]{2,1,0:T(8,128)(2,1)S(1)}) custom-call(s32[1,8]{1,0:T(1,128)S(1)} %copy-done.4, s32[1,32]{1,0:T(1,128)S(1)} %bitcast.6, bf16[128,2048]{1,0:T(8,128)(2,1)S(1)} %copy-done, bf16[4,32,2048]{2,1,0:T(8,128)(2,1)} %dx_hbm.1, bf16[544,2048]{1,0:T(8,128)(2,1)} %bitcast.7, bf16[128,2048]{1,0:T(8,128)(2,1)} %pg_hbm.1, ...), custom_call_target="tpu_custom_call" | custom-call | tf_op jit(solution)/shard_map/layer/pallas_call | solution.py:311
  53.9 0.8 %copy.16 = bf16[128,2048]{1,0:T(8,128)(2,1)} copy(bf16[128,2048]{1,0:T(8,128)(2,1)S(1)} %get-tuple-element.4) | data formatting | bytes 1048576
  54.7 0.8 %copy.17 = bf16[4,32,2048]{2,1,0:T(8,128)(2,1)} copy(bf16[4,32,2048]{2,1,0:T(8,128)(2,1)S(1)} %get-tuple-element.5) | data formatting | bytes 1048576
Async XLA Ops:
  0.6 1.0 %copy-start = (bf16[128,2048]{1,0:T(8,128)(2,1)S(1)}, bf16[128,2048]{1,0:T(8,128)(2,1)}, u32[]{:S(2)}) copy-start(bf16[128,2048]{1,0:T(8,128)(2,1)} %px_hbm.1) | copy-start | bytes 1572868
  1.7 0.9 %copy-start.1 = (f32[16,2048]{1,0:T(8,128)S(1)}, f32[16,2048]{1,0:T(8,128)}, u32[]{:S(2)}) copy-start(f32[16,2048]{1,0:T(8,128)} %alog_hbm.1) | copy-start | bytes 393220
  2.6 0.7 %copy-start.2 = (f32[2048]{0:T(1024)S(1)}, f32[2048]{0:T(1024)}, u32[]{:S(2)}) copy-start(f32[2048]{0:T(1024)} %param.21) | copy-start | bytes 24580
  3.3 0.7 %copy-start.3 = (f32[2048]{0:T(1024)S(1)}, f32[2048]{0:T(1024)}, u32[]{:S(2)}) copy-start(f32[2048]{0:T(1024)} %param.23) | copy-start | bytes 24580
  4.0 0.7 %copy-start.4 = (s32[1,8]{1,0:T(1,128)S(1)}, s32[1,8]{1,0:T(1,128)}, u32[]{:S(2)}) copy-start(s32[1,8]{1,0:T(1,128)} %len_hbm.1) | copy-start | bytes 100
  4.6 0.7 %copy-start.5 = (s32[32,1]{0,1:T(1,128)S(1)}, s32[32,1]{0,1:T(1,128)}, u32[]{:S(2)}) copy-start(s32[32,1]{0,1:T(1,128)} %param.15) | copy-start | bytes 388

commit v4 on v3

--- a/solution.py
+++ b/solution.py
@@ -59,8 +59,8 @@
              (skip_hbm, skip_ref))
         )
     ]
-    for load in loads:
-        load.start()
+    for i in (0, 1, 2, 7, 8, 9, 10, 11):
+        loads[i].start()
     barrier = pltpu.get_barrier_semaphore()
     for k in range(1, n):
         pl.semaphore_signal(barrier, inc=1, device_id={"tp": lax.rem(me + k, n)}, device_id_type=MESH)
@@ -113,6 +113,8 @@
             pl.semaphore_wait(barrier, n - 1 + ng - 1)
             for k in range(1, n):
                 scatter(phase, k).start()
+            for i in (3, 4, 5, 6):
+                loads[i].start()
     for i in range(7, 12):
         loads[i].wait()
 
@@ -244,6 +246,12 @@
             decay[i * SET:(i + 1) * SET, :] = step[i]
             forced[i] = forcing(1, (i * rows + base) // SET, step[i] * values[i])
         rates = -jnp.exp(alog_ref[:, lanes]) * LOG2E
+        if takes and base == 0:
+            for k in range(1, ng):
+                handoff(b, k).wait_recv()
+            for k in range(ng):
+                for r in range(cap):
+                    pool[k * cap + r] = state_in[b, k, r]
         for j in range(SET):
             row = base + j
             h = cache[row, :, lanes]
@@ -269,11 +277,6 @@
         return carry
 
     def late_block(b, carry):
-        for k in range(1, ng):
-            handoff(b, k).wait_recv()
-        for k in range(ng):
-            for r in range(cap):
-                pool[k * cap + r] = state_in[b, k, r]
         for base in late:
             decode_rows(b, base, True)
         return carry
@@ -301,7 +304,7 @@
     rank, states = dt_weight.shape[0], a_log.shape[0]
     width = xproj_weight.shape[1]
     cap = max(1, 2 * lengths.shape[1] // ng)
-    block = min(512, channels)
+    block = min(256, channels)
     blocks = channels // block
     piece = width // n
     columns = max(tokens, steps * rows)
@@ -353,7 +356,7 @@
             dma((blocks, ng - 1)),
         ],
         compiler_params=pltpu.CompilerParams(
-            collective_id=0, has_side_effects=True, vmem_limit_bytes=52 * 1024 * 1024
+            collective_id=0, has_side_effects=True, vmem_limit_bytes=63 * 1024 * 1024
         ),
         name="layer",
     )(lengths, routes.T, prefill_x, decode_x, xproj_weight.T, prefill_gate, decode_gate, cached_state, dt_weight,

time: 55.8 us -> 66.5 us (1.19)
  the two profiles are of different devices: /device:TPU:13 before, /device:TPU:14 now
where the time goes in v4:
time: 66.5 us; the launch traced here: 66.3 us
  Pallas kernels  61.9 us (93%)
  local copies, waits for them, and re-layouts  3.76 us (6%)
    pallas_call x1, Pallas kernels, local(): pl.pallas_call(functools.partial(kernel, n, ng, cap, block), out_shape=(j...  61.9 us
    unnamed x2, local copies, waits for them, and re-layouts  3.76 us

profile of v4, /device:TPU:14, one launch (start us, length us, event | category | flops | bytes accessed | tf_op | source)
XLA Modules:
  0.0 66.3 jit_solution(11441185577093937669)
XLA Ops:
  0.6 61.9 %layer.1 = (bf16[128,2048]{1,0:T(8,128)(2,1)}, bf16[4,32,2048]{2,1,0:T(8,128)(2,1)}) custom-call(s32[1,8]{1,0:T(1,128)} %len_hbm.1, s32[1,32]{1,0:T(1,128)} %bitcast.7, bf16[128,2048]{1,0:T(8,128)(2,1)} %px_hbm.1, bf16[4,32,2048]{2,1,0:T(8,128)(2,1)} %dx_hbm.1, bf16[544,2048]{1,0:T(8,128)(2,1)} %bitcast.4, bf16[128,2048]{1,0:T(8,128)(2,1)} %pg_hbm.1, ...), custom_call_target="tpu_custom_call" | custom-call | tf_op jit(solution)/shard_map/layer/pallas_call | solution.py:314
  62.5 1.9 %copy.16 = bf16[128,2048]{1,0:T(8,128)(2,1)} copy(bf16[128,2048]{1,0:T(8,128)(2,1)} %get-tuple-element.4) | data formatting | bytes 1048576
  64.4 1.9 %copy.17 = bf16[4,32,2048]{2,1,0:T(8,128)(2,1)} copy(bf16[4,32,2048]{2,1,0:T(8,128)(2,1)} %get-tuple-element.5) | data formatting | bytes 1048576

commit v5 on v4

--- a/solution.py
+++ b/solution.py
@@ -38,7 +38,7 @@
            bias_hbm, alog_hbm, skip_hbm, outp_ref, outd_ref,
            len_ref, routes_ref, bias_ref, alog_ref, skip_ref,
            px, dx, w, pg, dg, cache, dtw, part, recv, full, low, lhs_c, lhs_b,
-           decay, force, forced, hb, hd, mix, state_out, state_in, pool,
+           decay, forced, hb, hd, state_out, state_in, pool,
            in_sem, send_sem, recv_sem, gsend_sem, grecv_sem, hsend_sem, hrecv_sem):
     me = lax.axis_index("tp")
     group = lax.axis_index("group")
@@ -206,17 +206,17 @@
         step = step_sizes(0, lanes)
         values = px[:, lanes].astype(F32)
         decay[...] = jnp.where(first, 1e30, step)
-        force[...] = step * values
+        pushes = step * values
+        for s in range(tokens // SET):
+            forced[s] = forcing(0, s, pushes[s * SET:(s + 1) * SET])
         rates = -jnp.exp(alog_ref[:, lanes]) * LOG2E
 
         def some(s, h):
             base = pl.multiple_of(s * SET, SET)
-            forced[0] = forcing(0, s, force[pl.ds(base, SET), :])
             for j in range(SET):
                 da = jnp.exp2(decay[pl.ds(base + j, 1), :] * rates)
-                h = da * h + forced[0, j * states:(j + 1) * states, :]
+                h = da * h + forced[s, j * states:(j + 1) * states, :]
                 hb[base + j] = h.astype(BF16)
-            mix[pl.ds(base, SET), :] = readout(0, s, hb[pl.ds(base, SET)])
             return h
 
         lax.fori_loop(0, tokens // SET, some, jnp.zeros((states, block), F32))
@@ -226,7 +226,8 @@
             handoff(b, k).start()
         for r in range(cap):
             state_in[b, 0, r] = hb[leaving[0][r]].astype(F32)
-        outp_ref[:, lanes] = ((mix[...] + skip_ref[:, lanes] * values) * silu(pg[:, lanes].astype(F32))).astype(BF16)
+        mixed = jnp.concatenate([readout(0, s, hb[s * SET:(s + 1) * SET]) for s in range(tokens // SET)], axis=0)
+        outp_ref[:, lanes] = ((mixed + skip_ref[:, lanes] * values) * silu(pg[:, lanes].astype(F32))).astype(BF16)
         return carry
 
     lax.fori_loop(0, blocks // 2, prefill_block, 0)
@@ -304,7 +305,7 @@
     rank, states = dt_weight.shape[0], a_log.shape[0]
     width = xproj_weight.shape[1]
     cap = max(1, 2 * lengths.shape[1] // ng)
-    block = min(256, channels)
+    block = min(512, channels)
     blocks = channels // block
     piece = width // n
     columns = max(tokens, steps * rows)
@@ -339,11 +340,9 @@
             pltpu.VMEM((2, columns // SET, 2 * SET, SET * states), BF16),
             pltpu.VMEM((2, columns // SET, SET * states, 3 * SET), BF16),
             pltpu.VMEM((columns, block), F32),
-            pltpu.VMEM((columns, block), F32),
-            pltpu.VMEM((steps, SET * states, block), F32),
+            pltpu.VMEM((columns // SET, SET * states, block), F32),
             pltpu.VMEM((tokens, states, block), BF16),
             pltpu.VMEM((steps, SET, states, block), BF16),
-            pltpu.VMEM((tokens, block), F32),
             pltpu.VMEM((blocks, ng - 1, cap, states, block), F32),
             pltpu.VMEM((blocks, ng, cap, states, block), F32),
             pltpu.VMEM((ng * cap + lengths.shape[1], states, block), F32),
@@ -356,7 +355,7 @@
             dma((blocks, ng - 1)),
         ],
         compiler_params=pltpu.CompilerParams(
-            collective_id=0, has_side_effects=True, vmem_limit_bytes=63 * 1024 * 1024
+            collective_id=0, has_side_effects=True, vmem_limit_bytes=60 * 1024 * 1024
         ),
         name="layer",
     )(lengths, routes.T, prefill_x, decode_x, xproj_weight.T, prefill_gate, decode_gate, cached_state, dt_weight,

time: 66.5 us -> 51.9 us (0.78)
  the two profiles are of different devices: /device:TPU:14 before, /device:TPU:13 now
where the time goes in v5:
time: 51.9 us; the launch traced here: 51.7 us
  Pallas kernels  47.3 us (91%)
  local copies, waits for them, and re-layouts  3.76 us (7%)
  between operations  0.64 us (1%)
    pallas_call x1, Pallas kernels, local(): pl.pallas_call(functools.partial(kernel, n, ng, cap, block), out_shape=(j...  47.3 us
    unnamed x2, local copies, waits for them, and re-layouts  3.76 us

profile of v5, /device:TPU:13, one launch (start us, length us, event | category | flops | bytes accessed | tf_op | source)
XLA Modules:
  0.0 51.7 jit_solution(10856360034577018939)
XLA Ops:
  0.6 47.3 %layer.1 = (bf16[128,2048]{1,0:T(8,128)(2,1)}, bf16[4,32,2048]{2,1,0:T(8,128)(2,1)}) custom-call(s32[1,8]{1,0:T(1,128)} %len_hbm.1, s32[1,32]{1,0:T(1,128)} %bitcast.7, bf16[128,2048]{1,0:T(8,128)(2,1)} %px_hbm.1, bf16[4,32,2048]{2,1,0:T(8,128)(2,1)} %dx_hbm.1, bf16[544,2048]{1,0:T(8,128)(2,1)} %bitcast.4, bf16[128,2048]{1,0:T(8,128)(2,1)} %pg_hbm.1, ...), custom_call_target="tpu_custom_call" | custom-call | tf_op jit(solution)/shard_map/layer/pallas_call | solution.py:315
  48.0 1.9 %copy.16 = bf16[128,2048]{1,0:T(8,128)(2,1)} copy(bf16[128,2048]{1,0:T(8,128)(2,1)} %get-tuple-element.4) | data formatting | bytes 1048576
  49.9 1.9 %copy.17 = bf16[4,32,2048]{2,1,0:T(8,128)(2,1)} copy(bf16[4,32,2048]{2,1,0:T(8,128)(2,1)} %get-tuple-element.5) | data formatting | bytes 1048576

commit v6 on v5

--- a/solution.py
+++ b/solution.py
@@ -67,24 +67,49 @@
     for k in range(1, ng):
         pl.semaphore_signal(barrier, inc=1, device_id={"group": lax.rem(group + k, ng)}, device_id_type=MESH)
 
-    def scatter(phase, k):
-        peer = lax.rem(me + k, n)
+    half = n // 2
+    partner = me + 1 - 2 * lax.rem(me, 2)
+
+    def even(j):
+        return lax.rem(me + 2 * j, n)
+
+    def to_partner(phase, j):
         return pltpu.make_async_remote_copy(
-            src_ref=part.at[phase, peer],
-            dst_ref=recv.at[phase, k - 1],
-            send_sem=send_sem.at[phase, k - 1],
-            recv_sem=recv_sem.at[phase, k - 1],
-            device_id={"tp": peer},
+            src_ref=part.at[phase, lax.rem(partner + 2 * j, n)],
+            dst_ref=recv.at[phase, j],
+            send_sem=send_sem.at[phase, j],
+            recv_sem=recv_sem.at[phase, j],
+            device_id={"tp": partner},
             device_id_type=MESH,
         )
 
-    def gather(phase, k, owner):
+    def to_owner(phase, j):
+        return pltpu.make_async_remote_copy(
+            src_ref=part.at[phase, even(j)],
+            dst_ref=recv.at[phase, half + j - 1],
+            send_sem=send_sem.at[phase, half + j - 1],
+            recv_sem=recv_sem.at[phase, half + j - 1],
+            device_id={"tp": even(j)},
+            device_id_type=MESH,
+        )
+
+    def pair_up(phase):
+        for j in (*range(1, half), 0):
+            to_partner(phase, j).start()
+
+    def pass_on(phase):
+        for j in range(1, half):
+            to_partner(phase, j).wait_recv()
+            part[phase, even(j)] = part[phase, even(j)] + recv[phase, j]
+            to_owner(phase, j).start()
+
+    def gather(phase, place, owner, device):
         return pltpu.make_async_remote_copy(
             src_ref=full.at[phase, owner],
             dst_ref=full.at[phase, owner],
-            send_sem=gsend_sem.at[phase, k - 1],
-            recv_sem=grecv_sem.at[phase, k - 1],
-            device_id={"tp": lax.rem(me + k, n)},
+            send_sem=gsend_sem.at[phase, place],
+            recv_sem=grecv_sem.at[phase, place],
+            device_id={"tp": device},
             device_id_type=MESH,
         )
 
@@ -111,10 +136,10 @@
             part[phase, j] = res[j * piece:(j + 1) * piece]
         if phase == 0:
             pl.semaphore_wait(barrier, n - 1 + ng - 1)
-            for k in range(1, n):
-                scatter(phase, k).start()
+            pair_up(0)
             for i in (3, 4, 5, 6):
                 loads[i].start()
+    pass_on(0)
     for i in range(7, 12):
         loads[i].wait()
 
@@ -149,24 +174,30 @@
     taken, places = located[0], located[1:]
 
     def reduce(phase):
-        total = part[phase, me]
-        for k in range(1, n):
-            scatter(phase, k).wait_recv()
-            total = total + recv[phase, k - 1]
+        to_partner(phase, 0).wait_recv()
+        total = part[phase, me] + recv[phase, 0]
+        for j in range(1, half):
+            to_owner(phase, j).wait_recv()
+            total = total + recv[phase, half + j - 1]
         full[phase, me] = total
-        for k in range(1, n):
-            gather(phase, k, me).start()
+        for j in range(1, half):
+            gather(phase, 2 * j - 1, me, even(j)).start()
+        gather(phase, 0, me, partner).start()
 
     reduce(0)
-    for k in range(1, n):
-        scatter(1, k).start()
+    pair_up(1)
 
     tile = (lax.broadcasted_iota(jnp.int32, (states, SET * states), 1) % states
             == lax.broadcasted_iota(jnp.int32, (states, SET * states), 0)).astype(BF16)
 
     def collect(phase):
-        for k in range(1, n):
-            gather(phase, k, lax.rem(me + n - k, n)).wait_recv()
+        for j in range(1, half):
+            source = lax.rem(me + n - 2 * j, n)
+            gather(phase, 2 * j - 1, source, even(j)).wait_recv()
+            gather(phase, 2 * j, source, partner).start()
+        gather(phase, 0, partner, partner).wait_recv()
+        for j in range(1, half):
+            gather(phase, 2 * j, lax.rem(partner + n - 2 * j, n), partner).wait_recv()
         proj = jnp.concatenate([full[phase, j] for j in range(n)], axis=0)
         low[phase] = proj[:rank].astype(BF16)
         width = proj.shape[1]
@@ -194,6 +225,7 @@
         return softplus(dot_tn(low[phase], dtw[:, lanes]) + bias_ref[:, lanes])
 
     collect(0)
+    pass_on(1)
     loads[3].wait()
     loads[4].wait()
     position = lax.broadcasted_iota(jnp.int32, (tokens, block), 0)
@@ -286,9 +318,13 @@
     lax.fori_loop(0, blocks, late_block, 0)
 
     for phase in range(2):
-        for k in range(1, n):
-            scatter(phase, k).wait_send()
-            gather(phase, k, me).wait_send()
+        for j in range(half):
+            to_partner(phase, j).wait_send()
+        gather(phase, 0, me, partner).wait_send()
+        for j in range(1, half):
+            to_owner(phase, j).wait_send()
+            gather(phase, 2 * j - 1, me, even(j)).wait_send()
+            gather(phase, 2 * j, lax.rem(me + n - 2 * j, n), partner).wait_send()
 
     def finish(b, carry):
         for k in range(1, ng):

time: 51.9 us -> 52.2 us (level)
  the two profiles are of different devices: /device:TPU:13 before, /device:TPU:1 now
where the time goes in v6:
time: 52.2 us; the launch traced here: 52 us
  Pallas kernels  47.6 us (91%)
  local copies, waits for them, and re-layouts  3.76 us (7%)
  between operations  0.64 us (1%)
    pallas_call x1, Pallas kernels, local(): pl.pallas_call(functools.partial(kernel, n, ng, cap, block), out_shape=(j...  47.6 us
    unnamed x2, local copies, waits for them, and re-layouts  3.76 us

profile of v6, /device:TPU:1, one launch (start us, length us, event | category | flops | bytes accessed | tf_op | source)
XLA Modules:
  0.0 52.0 jit_solution(4514735872412125927)
XLA Ops:
  0.6 47.6 %layer.1 = (bf16[128,2048]{1,0:T(8,128)(2,1)}, bf16[4,32,2048]{2,1,0:T(8,128)(2,1)}) custom-call(s32[1,8]{1,0:T(1,128)} %len_hbm.1, s32[1,32]{1,0:T(1,128)} %bitcast.7, bf16[128,2048]{1,0:T(8,128)(2,1)} %px_hbm.1, bf16[4,32,2048]{2,1,0:T(8,128)(2,1)} %dx_hbm.1, bf16[544,2048]{1,0:T(8,128)(2,1)} %bitcast.4, bf16[128,2048]{1,0:T(8,128)(2,1)} %pg_hbm.1, ...), custom_call_target="tpu_custom_call" | custom-call | tf_op jit(solution)/shard_map/layer/pallas_call | solution.py:351
  48.2 1.9 %copy.16 = bf16[128,2048]{1,0:T(8,128)(2,1)} copy(bf16[128,2048]{1,0:T(8,128)(2,1)} %get-tuple-element.4) | data formatting | bytes 1048576
  50.1 1.9 %copy.17 = bf16[4,32,2048]{2,1,0:T(8,128)(2,1)} copy(bf16[4,32,2048]{2,1,0:T(8,128)(2,1)} %get-tuple-element.5) | data formatting | bytes 1048576
